TPU v7x, 512 devices: a whole 4x8x8 slice. The times are simulated.
512 devices in a mesh: blk: 32 (over x, y_lo, core), dp: 16 (over y_hi, z).
Axes of the slice: x: 4, y: 8 (y_hi: 2, y_lo: 4; y = y_hi * 4 + y_lo), z: 8, core: 2. Of those that a mesh axis runs over, the one named last changes fastest.
Arguments:
- image_emb: bfloat16 [16384, 1024], P(('blk', 'dp')), may hold values from -4 to 4
- text_emb: bfloat16 [16384, 1024], P(('blk', 'dp')), may hold values from -4 to 4
- labels: int32 [16384], P(('blk', 'dp')), may hold values from 0 to 16383, as said below
- logit_scale: float32 [], replicated, may hold values from 8 to 30
Outputs:
- grad_image: bfloat16 [16384, 1024], P(('blk', 'dp'))
- grad_text: bfloat16 [16384, 1024], P(('blk', 'dp'))
Inputs may be any that keep to these rules, and one draw needn't show every extreme that they name: labels is a permutation of 0 to 16383: the positive text of image i is text labels[i].
All inputs are finite; a program needn't handle non-finite values.
Results may differ from a plain program's by a relative error of at most 0.0085.
Values may be sent and summed in bfloat16 or wider, within the bound.
A program may use at most 64 MiB of HBM per device.

v0:
```python
import jax
import jax.numpy as jnp
from jax import lax
from jax.sharding import PartitionSpec as P


def merged(value, axis, join):
    pieces = jax.tree.map(lambda part: lax.all_gather(part, axis), value)
    head = jax.tree.map(lambda part: part[0], pieces)
    tail = jax.tree.map(lambda part: part[1:], pieces)
    total, _ = lax.scan(lambda total, share: (join(total, share), None), head, tail)
    return total


def shifted(block, axis, distance):
    devices = range(lax.axis_size(axis))
    route = [((i - distance) % len(devices), i) for i in devices]
    return lax.ppermute(block, axis, route)


def combine_totals(left_pair, right_pair):
    top_value = jnp.maximum(left_pair[0], right_pair[0])
    summed = left_pair[1] * jnp.exp(left_pair[0] - top_value) + right_pair[1] * jnp.exp(
        right_pair[0] - top_value
    )
    return (top_value, summed)


def per_device(image_emb, text_emb, labels, logit_scale):
    shard_rows = image_emb.shape[0]
    cycle_size = lax.axis_size("blk")
    cycle_index = lax.axis_index("blk")
    group_size = lax.axis_size("dp")
    group_index = lax.axis_index("dp")
    images, row_labels = (
        lax.all_gather(image_emb, "dp", axis=0, tiled=True),
        lax.all_gather(labels, "dp", axis=0, tiled=True),
    )
    collected = lax.all_gather(text_emb, "blk", axis=0, tiled=True)
    logits = logit_scale * lax.dot_general(
        collected, images, (((1,), (1,)), ((), ())), preferred_element_type=jnp.float32
    )
    row_max = jnp.max(logits, axis=0)
    row_total = jnp.sum(jnp.exp(logits - row_max[None, :]), axis=0)
    column_max = jnp.max(logits, axis=1)
    column_total = jnp.sum(jnp.exp(logits - column_max[:, None]), axis=1)
    row_max, row_total = merged((row_max, row_total), "dp", combine_totals)
    column_max, column_total = merged((column_max, column_total), "blk", combine_totals)
    row_lse = row_max + jnp.log(row_total)
    column_lse = column_max + jnp.log(column_total)
    text_slot = jnp.arange(collected.shape[0], dtype=jnp.int32)
    text_ids = (
        text_slot // shard_rows * group_size + group_index
    ) * shard_rows + text_slot % shard_rows
    target = (row_labels[None, :] == text_ids[:, None]).astype(jnp.float32)
    weights = (
        (jnp.exp(logits - row_lse[None, :]) + jnp.exp(logits - column_lse[:, None]) - 2.0 * target)
        * 0.5
    ).astype(jnp.bfloat16)
    grad_image = lax.psum_scatter(
        logit_scale
        * lax.dot_general(
            weights, collected, (((0,), (0,)), ((), ())), preferred_element_type=jnp.float32
        ),
        "dp",
        scatter_dimension=0,
        tiled=True,
    ).astype(jnp.bfloat16)

    def text_term(block_owner):
        weight_rows = lax.dynamic_slice_in_dim(weights, block_owner * shard_rows, shard_rows, 0)
        return logit_scale * jnp.dot(weight_rows, images, preferred_element_type=jnp.float32)

    empty = jnp.zeros((shard_rows, text_emb.shape[1]), jnp.float32)

    def carry_step(turn, carried):
        block_owner = (cycle_index - 1 - turn) % cycle_size
        carried = carried + text_term(block_owner)
        return shifted(carried, "blk", 1)

    carried = lax.fori_loop(0, cycle_size - 1, carry_step, empty)
    text_total = carried + text_term(cycle_index)
    return (grad_image, text_total.astype(jnp.bfloat16))


def solution(mesh):
    in_specs = (P(("blk", "dp"), None), P(("blk", "dp"), None), P(("blk", "dp")), P())
    out_specs = (P(("blk", "dp"), None), P(("blk", "dp"), None))
    return jax.shard_map(
        per_device, mesh=mesh, in_specs=in_specs, out_specs=out_specs, check_vma=False
    )
```

profile of v0, /device:TPU:1, one launch (start us, length us, event | category | flops | bytes accessed | tf_op | source)
XLA Modules:
  0.0 711.4 jit_solution(615991382331024100)
XLA Ops:
  12.1 23.3 %all-reduce = s32[512]{0:T(512)S(1)} all-reduce(s32[512]{0:T(512)S(1)} %dynamic-update-slice), channel_id=1, replica_groups=mesh['blk'=32,'dp'=16] {'dp'}, use_global_device_ids=true, to_apply=%add | all-reduce | flops 512 | bytes 4096
  35.5 66.5 %all-gather.11.cloned.1.call-done = bf16[512,1024]{1,0:T(8,128)(2,1)} async-done(((bf16[32,1024]{1,0:T(8,128)(2,1)}), bf16[512,1024]{1,0:T(8,128)(2,1)}) %all-gather.11.cloned.1.call-update) | async-done | bytes 1048592 | tf_op jit(solution)/shard_map/all_gather | solution.py:36
  101.9 66.0 %all-gather.9.cloned.1.call-done = bf16[1024,1024]{1,0:T(8,128)(2,1)} async-done(((bf16[32,1024]{1,0:T(8,128)(2,1)}), bf16[1024,1024]{1,0:T(8,128)(2,1)}) %all-gather.9.cloned.1.call-update) | async-done | bytes 2097168 | tf_op jit(solution)/shard_map/all_gather | solution.py:39
  172.1 45.6 %all-gather.5 = f32[16,1,512]{2,1,0:T(1,128)S(1)} all-gather(f32[1,1,512]{2,1,0:T(1,128)S(1)} %bitcast.40), channel_id=3, replica_groups=mesh['blk'=32,'dp'=16] {'dp'}, dimensions={0}, use_global_device_ids=true | all-gather | bytes 34816 | tf_op jit(solution)/shard_map/all_gather | solution.py:8
  217.7 38.8 %all-gather.4 = f32[16,1,512]{2,1,0:T(1,128)S(1)} all-gather(f32[1,1,512]{2,1,0:T(1,128)S(1)} %bitcast.39), channel_id=2, replica_groups=mesh['blk'=32,'dp'=16] {'dp'}, dimensions={0}, use_global_device_ids=true | all-gather | bytes 34816 | tf_op jit(solution)/shard_map/all_gather | solution.py:8
  256.5 54.9 %all-gather.3 = f32[32768]{0:T(1024)S(1)} all-gather(f32[1024]{0:T(1024)S(1)} %get-tuple-element.222), channel_id=5, replica_groups=mesh['blk'=32,'dp'=16] {'blk'}, dimensions={0}, use_global_device_ids=true | all-gather | bytes 135168 | tf_op jit(solution)/shard_map/all_gather | solution.py:8
  311.5 38.4 %all-gather.2 = f32[32768]{0:T(1024)S(1)} all-gather(f32[1024]{0:T(1024)S(1)} %get-tuple-element.224), channel_id=4, replica_groups=mesh['blk'=32,'dp'=16] {'blk'}, dimensions={0}, use_global_device_ids=true | all-gather | bytes 135168 | tf_op jit(solution)/shard_map/all_gather | solution.py:8
  357.9 344.5 %while.41 = (s32[]{:T(128)}, f32[32,1024]{1,0:T(8,128)S(1)}, f32[]{:T(128)}, s32[]{:T(128)}, bf16[1024,512]{1,0:T(8,128)(2,1)S(1)}, /*index=5*/bf16[512,1024]{1,...) while((s32[]{:T(128)}, f32[32,1024]{1,0:T(8,128)S(1)}, f32[]{:T(128)}, ...), condition=%wide.region_10.11_spmd, body=%wide.region_9.10_spmd.sunk | while | flops 33619984 | bytes 1868100 | solution.py:81
  388.1 8.6 %collective-permute-done = f32[32,1024]{1,0:T(8,128)S(1)} collective-permute-done((f32[32,1024]{1,0:T(8,128)S(1)}, f32[32,1024]{1,0:T(8,128)S(1)}, u32[]{:S(2)}, u32[]{:S(2)}) %collective-permute-start) | collective-permute-done | bytes 131104 | tf_op jit(solution)/shard_map/while/body/eval_jaxpr/ppermute | solution.py:18
  399.6 8.3 %collective-permute-done = f32[32,1024]{1,0:T(8,128)S(1)} collective-permute-done((f32[32,1024]{1,0:T(8,128)S(1)}, f32[32,1024]{1,0:T(8,128)S(1)}, u32[]{:S(2)}, u32[]{:S(2)}) %collective-permute-start) | collective-permute-done | bytes 131104 | tf_op jit(solution)/shard_map/while/body/eval_jaxpr/ppermute | solution.py:18
  410.7 8.8 %collective-permute-done = f32[32,1024]{1,0:T(8,128)S(1)} collective-permute-done((f32[32,1024]{1,0:T(8,128)S(1)}, f32[32,1024]{1,0:T(8,128)S(1)}, u32[]{:S(2)}, u32[]{:S(2)}) %collective-permute-start) | collective-permute-done | bytes 131104 | tf_op jit(solution)/shard_map/while/body/eval_jaxpr/ppermute | solution.py:18
  422.4 8.5 %collective-permute-done = f32[32,1024]{1,0:T(8,128)S(1)} collective-permute-done((f32[32,1024]{1,0:T(8,128)S(1)}, f32[32,1024]{1,0:T(8,128)S(1)}, u32[]{:S(2)}, u32[]{:S(2)}) %collective-permute-start) | collective-permute-done | bytes 131104 | tf_op jit(solution)/shard_map/while/body/eval_jaxpr/ppermute | solution.py:18
  433.8 8.6 %collective-permute-done = f32[32,1024]{1,0:T(8,128)S(1)} collective-permute-done((f32[32,1024]{1,0:T(8,128)S(1)}, f32[32,1024]{1,0:T(8,128)S(1)}, u32[]{:S(2)}, u32[]{:S(2)}) %collective-permute-start) | collective-permute-done | bytes 131104 | tf_op jit(solution)/shard_map/while/body/eval_jaxpr/ppermute | solution.py:18
  445.2 8.8 %collective-permute-done = f32[32,1024]{1,0:T(8,128)S(1)} collective-permute-done((f32[32,1024]{1,0:T(8,128)S(1)}, f32[32,1024]{1,0:T(8,128)S(1)}, u32[]{:S(2)}, u32[]{:S(2)}) %collective-permute-start) | collective-permute-done | bytes 131104 | tf_op jit(solution)/shard_map/while/body/eval_jaxpr/ppermute | solution.py:18
  456.8 8.9 %collective-permute-done = f32[32,1024]{1,0:T(8,128)S(1)} collective-permute-done((f32[32,1024]{1,0:T(8,128)S(1)}, f32[32,1024]{1,0:T(8,128)S(1)}, u32[]{:S(2)}, u32[]{:S(2)}) %collective-permute-start) | collective-permute-done | bytes 131104 | tf_op jit(solution)/shard_map/while/body/eval_jaxpr/ppermute | solution.py:18
  468.6 8.9 %collective-permute-done = f32[32,1024]{1,0:T(8,128)S(1)} collective-permute-done((f32[32,1024]{1,0:T(8,128)S(1)}, f32[32,1024]{1,0:T(8,128)S(1)}, u32[]{:S(2)}, u32[]{:S(2)}) %collective-permute-start) | collective-permute-done | bytes 131104 | tf_op jit(solution)/shard_map/while/body/eval_jaxpr/ppermute | solution.py:18
  480.3 9.3 %collective-permute-done = f32[32,1024]{1,0:T(8,128)S(1)} collective-permute-done((f32[32,1024]{1,0:T(8,128)S(1)}, f32[32,1024]{1,0:T(8,128)S(1)}, u32[]{:S(2)}, u32[]{:S(2)}) %collective-permute-start) | collective-permute-done | bytes 131104 | tf_op jit(solution)/shard_map/while/body/eval_jaxpr/ppermute | solution.py:18
  492.5 8.6 %collective-permute-done = f32[32,1024]{1,0:T(8,128)S(1)} collective-permute-done((f32[32,1024]{1,0:T(8,128)S(1)}, f32[32,1024]{1,0:T(8,128)S(1)}, u32[]{:S(2)}, u32[]{:S(2)}) %collective-permute-start) | collective-permute-done | bytes 131104 | tf_op jit(solution)/shard_map/while/body/eval_jaxpr/ppermute | solution.py:18
  504.0 8.6 %collective-permute-done = f32[32,1024]{1,0:T(8,128)S(1)} collective-permute-done((f32[32,1024]{1,0:T(8,128)S(1)}, f32[32,1024]{1,0:T(8,128)S(1)}, u32[]{:S(2)}, u32[]{:S(2)}) %collective-permute-start) | collective-permute-done | bytes 131104 | tf_op jit(solution)/shard_map/while/body/eval_jaxpr/ppermute | solution.py:18
  515.4 8.6 %collective-permute-done = f32[32,1024]{1,0:T(8,128)S(1)} collective-permute-done((f32[32,1024]{1,0:T(8,128)S(1)}, f32[32,1024]{1,0:T(8,128)S(1)}, u32[]{:S(2)}, u32[]{:S(2)}) %collective-permute-start) | collective-permute-done | bytes 131104 | tf_op jit(solution)/shard_map/while/body/eval_jaxpr/ppermute | solution.py:18
  538.1 8.3 %collective-permute-done = f32[32,1024]{1,0:T(8,128)S(1)} collective-permute-done((f32[32,1024]{1,0:T(8,128)S(1)}, f32[32,1024]{1,0:T(8,128)S(1)}, u32[]{:S(2)}, u32[]{:S(2)}) %collective-permute-start) | collective-permute-done | bytes 131104 | tf_op jit(solution)/shard_map/while/body/eval_jaxpr/ppermute | solution.py:18
  549.2 8.5 %collective-permute-done = f32[32,1024]{1,0:T(8,128)S(1)} collective-permute-done((f32[32,1024]{1,0:T(8,128)S(1)}, f32[32,1024]{1,0:T(8,128)S(1)}, u32[]{:S(2)}, u32[]{:S(2)}) %collective-permute-start) | collective-permute-done | bytes 131104 | tf_op jit(solution)/shard_map/while/body/eval_jaxpr/ppermute | solution.py:18
  582.9 8.3 %collective-permute-done = f32[32,1024]{1,0:T(8,128)S(1)} collective-permute-done((f32[32,1024]{1,0:T(8,128)S(1)}, f32[32,1024]{1,0:T(8,128)S(1)}, u32[]{:S(2)}, u32[]{:S(2)}) %collective-permute-start) | collective-permute-done | bytes 131104 | tf_op jit(solution)/shard_map/while/body/eval_jaxpr/ppermute | solution.py:18
  683.0 8.3 %collective-permute-done = f32[32,1024]{1,0:T(8,128)S(1)} collective-permute-done((f32[32,1024]{1,0:T(8,128)S(1)}, f32[32,1024]{1,0:T(8,128)S(1)}, u32[]{:S(2)}, u32[]{:S(2)}) %collective-permute-start) | collective-permute-done | bytes 131104 | tf_op jit(solution)/shard_map/while/body/eval_jaxpr/ppermute | solution.py:18
  (207 shorter events, 225.7 us)
Async XLA Ops:
  7.2 94.8 %all-gather.11.cloned.1.call-start = ((), (), s32[]{:S(2)}) async-start(), calls=%async_computation.2 | async-start | bytes 1114112 | tf_op jit(solution)/shard_map/all_gather | solution.py:36
  7.9 160.0 %all-gather.9.cloned.1.call-start = ((), (), s32[]{:S(2)}) async-start(), calls=%async_computation.1 | async-start | bytes 2162688 | tf_op jit(solution)/shard_map/all_gather | solution.py:39
  8.6 694.7 %reduce-scatter.2.cloned.1.call-start = ((), (), s32[]{:S(2)}) async-start(), calls=%async_computation.3 | async-start | bytes 2228224 | tf_op jit(solution)/shard_map/reduce_scatter | solution.py:60
  375.1 10.2 %collective-permute-start = (f32[32,1024]{1,0:T(8,128)S(1)}, f32[32,1024]{1,0:T(8,128)S(1)}, u32[]{:S(2)}, u32[]{:S(2)}) collective-permute-start(f32[32,1024]{1,0:T(8,128)S(1)} %fusion.30), channel_id=1, source_target_pairs={{496,0},{0,16},{16,32},{32,48},{48,64},{64,80},{80,96},{96,112},{1... | collective-permute-start | bytes 393224 | tf_op jit(solution)/shard_map/while/body/eval_jaxpr/ppermute | solution.py:18
  386.2 10.5 %collective-permute-start = (f32[32,1024]{1,0:T(8,128)S(1)}, f32[32,1024]{1,0:T(8,128)S(1)}, u32[]{:S(2)}, u32[]{:S(2)}) collective-permute-start(f32[32,1024]{1,0:T(8,128)S(1)} %fusion.30), channel_id=1, source_target_pairs={{496,0},{0,16},{16,32},{32,48},{48,64},{64,80},{80,96},{96,112},{1... | collective-permute-start | bytes 393224 | tf_op jit(solution)/shard_map/while/body/eval_jaxpr/ppermute | solution.py:18
  397.7 10.2 %collective-permute-start = (f32[32,1024]{1,0:T(8,128)S(1)}, f32[32,1024]{1,0:T(8,128)S(1)}, u32[]{:S(2)}, u32[]{:S(2)}) collective-permute-start(f32[32,1024]{1,0:T(8,128)S(1)} %fusion.30), channel_id=1, source_target_pairs={{496,0},{0,16},{16,32},{32,48},{48,64},{64,80},{80,96},{96,112},{1... | collective-permute-start | bytes 393224 | tf_op jit(solution)/shard_map/while/body/eval_jaxpr/ppermute | solution.py:18
  408.8 10.7 %collective-permute-start = (f32[32,1024]{1,0:T(8,128)S(1)}, f32[32,1024]{1,0:T(8,128)S(1)}, u32[]{:S(2)}, u32[]{:S(2)}) collective-permute-start(f32[32,1024]{1,0:T(8,128)S(1)} %fusion.30), channel_id=1, source_target_pairs={{496,0},{0,16},{16,32},{32,48},{48,64},{64,80},{80,96},{96,112},{1... | collective-permute-start | bytes 393224 | tf_op jit(solution)/shard_map/while/body/eval_jaxpr/ppermute | solution.py:18
  420.4 10.5 %collective-permute-start = (f32[32,1024]{1,0:T(8,128)S(1)}, f32[32,1024]{1,0:T(8,128)S(1)}, u32[]{:S(2)}, u32[]{:S(2)}) collective-permute-start(f32[32,1024]{1,0:T(8,128)S(1)} %fusion.30), channel_id=1, source_target_pairs={{496,0},{0,16},{16,32},{32,48},{48,64},{64,80},{80,96},{96,112},{1... | collective-permute-start | bytes 393224 | tf_op jit(solution)/shard_map/while/body/eval_jaxpr/ppermute | solution.py:18
  431.8 10.5 %collective-permute-start = (f32[32,1024]{1,0:T(8,128)S(1)}, f32[32,1024]{1,0:T(8,128)S(1)}, u32[]{:S(2)}, u32[]{:S(2)}) collective-permute-start(f32[32,1024]{1,0:T(8,128)S(1)} %fusion.30), channel_id=1, source_target_pairs={{496,0},{0,16},{16,32},{32,48},{48,64},{64,80},{80,96},{96,112},{1... | collective-permute-start | bytes 393224 | tf_op jit(solution)/shard_map/while/body/eval_jaxpr/ppermute | solution.py:18
  443.3 10.7 %collective-permute-start = (f32[32,1024]{1,0:T(8,128)S(1)}, f32[32,1024]{1,0:T(8,128)S(1)}, u32[]{:S(2)}, u32[]{:S(2)}) collective-permute-start(f32[32,1024]{1,0:T(8,128)S(1)} %fusion.30), channel_id=1, source_target_pairs={{496,0},{0,16},{16,32},{32,48},{48,64},{64,80},{80,96},{96,112},{1... | collective-permute-start | bytes 393224 | tf_op jit(solution)/shard_map/while/body/eval_jaxpr/ppermute | solution.py:18
  454.9 10.8 %collective-permute-start = (f32[32,1024]{1,0:T(8,128)S(1)}, f32[32,1024]{1,0:T(8,128)S(1)}, u32[]{:S(2)}, u32[]{:S(2)}) collective-permute-start(f32[32,1024]{1,0:T(8,128)S(1)} %fusion.30), channel_id=1, source_target_pairs={{496,0},{0,16},{16,32},{32,48},{48,64},{64,80},{80,96},{96,112},{1... | collective-permute-start | bytes 393224 | tf_op jit(solution)/shard_map/while/body/eval_jaxpr/ppermute | solution.py:18
  466.6 10.8 %collective-permute-start = (f32[32,1024]{1,0:T(8,128)S(1)}, f32[32,1024]{1,0:T(8,128)S(1)}, u32[]{:S(2)}, u32[]{:S(2)}) collective-permute-start(f32[32,1024]{1,0:T(8,128)S(1)} %fusion.30), channel_id=1, source_target_pairs={{496,0},{0,16},{16,32},{32,48},{48,64},{64,80},{80,96},{96,112},{1... | collective-permute-start | bytes 393224 | tf_op jit(solution)/shard_map/while/body/eval_jaxpr/ppermute | solution.py:18
  478.4 11.2 %collective-permute-start = (f32[32,1024]{1,0:T(8,128)S(1)}, f32[32,1024]{1,0:T(8,128)S(1)}, u32[]{:S(2)}, u32[]{:S(2)}) collective-permute-start(f32[32,1024]{1,0:T(8,128)S(1)} %fusion.30), channel_id=1, source_target_pairs={{496,0},{0,16},{16,32},{32,48},{48,64},{64,80},{80,96},{96,112},{1... | collective-permute-start | bytes 393224 | tf_op jit(solution)/shard_map/while/body/eval_jaxpr/ppermute | solution.py:18
  490.6 10.5 %collective-permute-start = (f32[32,1024]{1,0:T(8,128)S(1)}, f32[32,1024]{1,0:T(8,128)S(1)}, u32[]{:S(2)}, u32[]{:S(2)}) collective-permute-start(f32[32,1024]{1,0:T(8,128)S(1)} %fusion.30), channel_id=1, source_target_pairs={{496,0},{0,16},{16,32},{32,48},{48,64},{64,80},{80,96},{96,112},{1... | collective-permute-start | bytes 393224 | tf_op jit(solution)/shard_map/while/body/eval_jaxpr/ppermute | solution.py:18
  502.0 10.5 %collective-permute-start = (f32[32,1024]{1,0:T(8,128)S(1)}, f32[32,1024]{1,0:T(8,128)S(1)}, u32[]{:S(2)}, u32[]{:S(2)}) collective-permute-start(f32[32,1024]{1,0:T(8,128)S(1)} %fusion.30), channel_id=1, source_target_pairs={{496,0},{0,16},{16,32},{32,48},{48,64},{64,80},{80,96},{96,112},{1... | collective-permute-start | bytes 393224 | tf_op jit(solution)/shard_map/while/body/eval_jaxpr/ppermute | solution.py:18
  513.5 10.5 %collective-permute-start = (f32[32,1024]{1,0:T(8,128)S(1)}, f32[32,1024]{1,0:T(8,128)S(1)}, u32[]{:S(2)}, u32[]{:S(2)}) collective-permute-start(f32[32,1024]{1,0:T(8,128)S(1)} %fusion.30), channel_id=1, source_target_pairs={{496,0},{0,16},{16,32},{32,48},{48,64},{64,80},{80,96},{96,112},{1... | collective-permute-start | bytes 393224 | tf_op jit(solution)/shard_map/while/body/eval_jaxpr/ppermute | solution.py:18
  525.0 10.2 %collective-permute-start = (f32[32,1024]{1,0:T(8,128)S(1)}, f32[32,1024]{1,0:T(8,128)S(1)}, u32[]{:S(2)}, u32[]{:S(2)}) collective-permute-start(f32[32,1024]{1,0:T(8,128)S(1)} %fusion.30), channel_id=1, source_target_pairs={{496,0},{0,16},{16,32},{32,48},{48,64},{64,80},{80,96},{96,112},{1... | collective-permute-start | bytes 393224 | tf_op jit(solution)/shard_map/while/body/eval_jaxpr/ppermute | solution.py:18
  536.1 10.2 %collective-permute-start = (f32[32,1024]{1,0:T(8,128)S(1)}, f32[32,1024]{1,0:T(8,128)S(1)}, u32[]{:S(2)}, u32[]{:S(2)}) collective-permute-start(f32[32,1024]{1,0:T(8,128)S(1)} %fusion.30), channel_id=1, source_target_pairs={{496,0},{0,16},{16,32},{32,48},{48,64},{64,80},{80,96},{96,112},{1... | collective-permute-start | bytes 393224 | tf_op jit(solution)/shard_map/while/body/eval_jaxpr/ppermute | solution.py:18
  547.3 10.5 %collective-permute-start = (f32[32,1024]{1,0:T(8,128)S(1)}, f32[32,1024]{1,0:T(8,128)S(1)}, u32[]{:S(2)}, u32[]{:S(2)}) collective-permute-start(f32[32,1024]{1,0:T(8,128)S(1)} %fusion.30), channel_id=1, source_target_pairs={{496,0},{0,16},{16,32},{32,48},{48,64},{64,80},{80,96},{96,112},{1... | collective-permute-start | bytes 393224 | tf_op jit(solution)/shard_map/while/body/eval_jaxpr/ppermute | solution.py:18
  580.9 10.2 %collective-permute-start = (f32[32,1024]{1,0:T(8,128)S(1)}, f32[32,1024]{1,0:T(8,128)S(1)}, u32[]{:S(2)}, u32[]{:S(2)}) collective-permute-start(f32[32,1024]{1,0:T(8,128)S(1)} %fusion.30), channel_id=1, source_target_pairs={{496,0},{0,16},{16,32},{32,48},{48,64},{64,80},{80,96},{96,112},{1... | collective-permute-start | bytes 393224 | tf_op jit(solution)/shard_map/while/body/eval_jaxpr/ppermute | solution.py:18
  592.0 10.2 %collective-permute-start = (f32[32,1024]{1,0:T(8,128)S(1)}, f32[32,1024]{1,0:T(8,128)S(1)}, u32[]{:S(2)}, u32[]{:S(2)}) collective-permute-start(f32[32,1024]{1,0:T(8,128)S(1)} %fusion.30), channel_id=1, source_target_pairs={{496,0},{0,16},{16,32},{32,48},{48,64},{64,80},{80,96},{96,112},{1... | collective-permute-start | bytes 393224 | tf_op jit(solution)/shard_map/while/body/eval_jaxpr/ppermute | solution.py:18
  636.6 10.2 %collective-permute-start = (f32[32,1024]{1,0:T(8,128)S(1)}, f32[32,1024]{1,0:T(8,128)S(1)}, u32[]{:S(2)}, u32[]{:S(2)}) collective-permute-start(f32[32,1024]{1,0:T(8,128)S(1)} %fusion.30), channel_id=1, source_target_pairs={{496,0},{0,16},{16,32},{32,48},{48,64},{64,80},{80,96},{96,112},{1... | collective-permute-start | bytes 393224 | tf_op jit(solution)/shard_map/while/body/eval_jaxpr/ppermute | solution.py:18
  669.9 10.2 %collective-permute-start = (f32[32,1024]{1,0:T(8,128)S(1)}, f32[32,1024]{1,0:T(8,128)S(1)}, u32[]{:S(2)}, u32[]{:S(2)}) collective-permute-start(f32[32,1024]{1,0:T(8,128)S(1)} %fusion.30), channel_id=1, source_target_pairs={{496,0},{0,16},{16,32},{32,48},{48,64},{64,80},{80,96},{96,112},{1... | collective-permute-start | bytes 393224 | tf_op jit(solution)/shard_map/while/body/eval_jaxpr/ppermute | solution.py:18
  681.1 10.2 %collective-permute-start = (f32[32,1024]{1,0:T(8,128)S(1)}, f32[32,1024]{1,0:T(8,128)S(1)}, u32[]{:S(2)}, u32[]{:S(2)}) collective-permute-start(f32[32,1024]{1,0:T(8,128)S(1)} %fusion.30), channel_id=1, source_target_pairs={{496,0},{0,16},{16,32},{32,48},{48,64},{64,80},{80,96},{96,112},{1... | collective-permute-start | bytes 393224 | tf_op jit(solution)/shard_map/while/body/eval_jaxpr/ppermute | solution.py:18
  (12 other events, 98.7 us)
Sparse Core Ops, SparseCore 0:
  11.2 90.7 all-gather.10
  104.1 63.8 all-gather.8
  356.8 212.1 reduce-scatter.1
where the time goes:
time: 718 us; the launch traced here: 711 us
  waiting for transfers between devices  385 us (54%)
  blocking collectives  201 us (28%)
  starting transfers between devices  63.7 us (9%)
  matrix products  35.6 us (5%)
  between operations  15.2 us (2%)
    ppermute x31, waiting for transfers between devices, shifted(): return lax.ppermute(block, axis, route)  252 us
    all_gather x4, blocking collectives, merged(): pieces = jax.tree.map(lambda part: lax.all_gather(part, axis), value)  178 us
    all_gather x1, waiting for transfers between devices, per_device(): lax.all_gather(image_emb, 'dp', axis=0, tiled=True)  66.5 us
    all_gather x1, waiting for transfers between devices, per_device(): collected = lax.all_gather(text_emb, 'blk', axis=0, tiled=True)  66 us
    ppermute x31, starting transfers between devices, shifted(): return lax.ppermute(block, axis, route)  63.6 us
    dot_general x32, matrix products, text_term(): jnp.dot(weight_rows, images, preferred_element_type=jnp.float32)  29.7 us
    unnamed x1, blocking collectives  23.3 us
  transfers between devices with their start and end apart: 34, of which 33 were waited for; matrix products, arithmetic and copies ran while one was open for 4% of the time, Pallas kernels for 0%

commit v1 on v0

v1 whole, which is shorter than its diff:
```python
import jax
import jax.numpy as jnp
from jax import lax
from jax.experimental import pallas as pl
from jax.experimental.pallas import tpu as pltpu
from jax.sharding import PartitionSpec as P

R = 32
E = 1024
W = E + 128
RING = 8
HALF = RING * 2 * R
SIGNS = (1, -1)
F32 = jnp.float32
BF16 = jnp.bfloat16


def hops(d, q):
    return 4 if d == q else 3


def lse2(a, b):
    top = jnp.maximum(a, b)
    return top + jnp.log(jnp.exp(a - top) + jnp.exp(b - top))


def rows_at(slot, count=R):
    return pl.ds(pl.multiple_of(slot * R, R), count)


def kernel(
    image_ref, text_ref, label_ref, scale_ref, out_image_ref, out_text_ref,
    images, texts, logits, wts, wts_t, grad_i, grad_t, row_stat, col_stat,
    row_vec, row_pair, row_ring, col_vec, col_pair, col_ring,
    swap_out, swap_in, stage, landed, last_out, last_in,
    pair_send, pair_recv, ring_send, ring_recv, sib_send, sib_recv,
    stat_send, stat_recv, srow_send, srow_recv, scol_send, scol_recv,
    swap_send, swap_recv, rs_send, rs_recv, last_send, last_recv,
):
    blk, dp = lax.axis_index("blk"), lax.axis_index("dp")
    core, x = blk % 2, blk // 8
    y, z = (dp // 8) * 4 + (blk // 2) % 4, dp % 8
    p = x % 2
    xa = x + 1 - 2 * p
    xb = (x + 2 * p + 3) % 4

    def at(x=x, y=y, z=z, core=core):
        return {"blk": (x * 4 + y % 4) * 2 + core, "dp": (y // 4) * 8 + z}

    def up(v, k):
        return (v + k + RING) % RING

    image_pair, text_pair, sibling = at(x=xa), at(x=xb), at(core=1 - core)
    diagonal = at(x=xb, core=1 - core)
    z_peers = [at(z=up(z, k)) for k in range(1, RING)]
    y_peers = [at(y=up(y, k)) for k in range(1, RING)]
    peers = [image_pair, text_pair, sibling, diagonal] + z_peers + y_peers

    barrier = pltpu.get_barrier_semaphore()
    for peer in peers:
        pl.semaphore_signal(barrier, inc=1, device_id=peer, device_id_type=pl.DeviceIdType.MESH)
    pl.semaphore_wait(barrier, len(peers))

    sent = []

    def copy(src, dst, ssem, rsem, peer):
        return pltpu.make_async_remote_copy(
            src_ref=src, dst_ref=dst, send_sem=ssem, recv_sem=rsem,
            device_id=peer, device_id_type=pl.DeviceIdType.MESH,
        )

    def send(src, dst, ssem, rsem, peer):
        one = copy(src, dst, ssem, rsem, peer)
        one.start()
        sent.append(one)

    def arrived(dst, ssem, rsem, peer):
        copy(dst, dst, ssem, rsem, peer).wait_recv()

    place, pair = (z, y), (image_pair, text_pair)
    ahead = [[at(z=up(z, s)) for s in SIGNS], [at(y=up(y, s)) for s in SIGNS]]

    def shard(kind, where, q):
        slot = where * 2 + (p if q == 0 else 1 - p)
        return (images if kind == 0 else texts).at[rows_at(slot)]

    def to_pair(kind):
        own = shard(kind, place[kind], 0)
        send(own, own, pair_send.at[kind], pair_recv.at[kind], pair[kind])

    def to_ring(kind, d, q, k):
        part = shard(kind, up(place[kind], -SIGNS[d] * (k - 1)), q)
        send(part, part, ring_send.at[kind, d, q, k - 1], ring_recv.at[kind, d, q, k - 1], ahead[kind][d])

    def sibling_slots(where, q):
        slot = where * 2 + (p if q == 0 else 1 - p)
        return texts.at[rows_at(slot)], texts.at[rows_at(slot + 2 * RING)]

    def to_sibling(step, where, q):
        mine, theirs = sibling_slots(where, q)
        send(mine, theirs, sib_send.at[q, step], sib_recv.at[q, step], sibling)

    digits = jnp.zeros((R, 128), jnp.int32)
    row_of = lax.broadcasted_iota(jnp.int32, (R, 128), 0)
    for r in range(R):
        digits = jnp.where(row_of == r, label_ref[r], digits)
    lane = lax.broadcasted_iota(jnp.int32, (R, 128), 1)
    digits = jnp.where(lane < 64, digits >> 7, digits & 127)
    own_image = rows_at(z * 2 + p)
    images[own_image, :E] = image_ref[...]
    images[own_image, E:] = digits.astype(F32).astype(BF16)
    texts[rows_at(y * 2 + p), :] = text_ref[...]

    for kind in range(2):
        for d in range(2):
            to_ring(kind, d, 0, 1)
        to_pair(kind)
    to_sibling(0, y, 0)
    for kind in range(2):
        arrived(shard(kind, place[kind], 1), pair_send.at[kind], pair_recv.at[kind], pair[kind])
        for d in range(2):
            to_ring(kind, d, 1, 1)
    to_sibling(0, y, 1)
    order = [(0, 0), (1, 0), (0, 1), (1, 1)]
    for k in range(1, 5):
        for d, q in order:
            if k > hops(d, q):
                continue
            for kind in range(2):
                where = up(place[kind], -SIGNS[d] * k)
                arrived(
                    shard(kind, where, q), ring_send.at[kind, d, q, k - 1],
                    ring_recv.at[kind, d, q, k - 1], ahead[kind][d],
                )
                if k < hops(d, q):
                    to_ring(kind, d, q, k + 1)
                if kind == 1:
                    to_sibling(k if d == 0 else RING - k, where, q)
    for q in range(2):
        for step in range(RING):
            arrived(sibling_slots(up(y, -step), q)[1], sib_send.at[q, step], sib_recv.at[q, step], sibling)

    scale = scale_ref[0]

    @pl.loop(0, 4)
    def _(n):
        cols = pl.ds(pl.multiple_of(n * 256, 256), 256)
        tile = scale * lax.dot_general(
            images[:, :E], texts[cols, :], (((1,), (1,)), ((), ())), preferred_element_type=F32
        )
        logits[:, cols] = tile
        top = jnp.max(tile, axis=0, keepdims=True)
        total = jnp.sum(jnp.exp(tile - top), axis=0, keepdims=True)
        col_vec[:, cols] = top + jnp.log(total)

    @pl.loop(0, 8)
    def _(n):
        rows = pl.ds(pl.multiple_of(n * 64, 64), 64)
        tile = logits[rows, :]
        top = jnp.max(tile, axis=1, keepdims=True)
        total = jnp.sum(jnp.exp(tile - top), axis=1, keepdims=True)
        row_stat[rows, :] = jnp.broadcast_to(top + jnp.log(total), (64, 128))

    row_vec[...] = jnp.transpose(row_stat[...])[0:1, :]

    send(row_vec, row_pair, stat_send.at[0], stat_recv.at[0], image_pair)
    col_peers = [text_pair, sibling, diagonal]
    for i, peer in enumerate(col_peers):
        send(col_vec, col_pair.at[i], stat_send.at[i + 1], stat_recv.at[i + 1], peer)
    arrived(row_pair, stat_send.at[0], stat_recv.at[0], image_pair)
    row_ring[0] = lse2(row_vec[...], row_pair[...])
    for k in range(1, RING):
        send(row_ring.at[0], row_ring.at[k], srow_send.at[k], srow_recv.at[k], z_peers[k - 1])
    for i, peer in enumerate(col_peers):
        arrived(col_pair.at[i], stat_send.at[i + 1], stat_recv.at[i + 1], peer)
    same = lse2(col_vec[...], col_pair[0])
    other = lse2(col_pair[1], col_pair[2])
    other = jnp.concatenate([other[:, HALF:], other[:, :HALF]], axis=1)
    col_ring[0] = lse2(same, other)
    for k in range(1, RING):
        send(col_ring.at[0], col_ring.at[k], scol_send.at[k], scol_recv.at[k], y_peers[k - 1])
    for k in range(1, RING):
        arrived(row_ring.at[k], srow_send.at[k], srow_recv.at[k], z_peers[k - 1])

    def joined(ring):
        parts = [ring[k] for k in range(RING)]
        top = parts[0]
        for part in parts[1:]:
            top = jnp.maximum(top, part)
        total = jnp.exp(parts[0] - top)
        for part in parts[1:]:
            total = total + jnp.exp(part - top)
        return top + jnp.log(total)

    row_stat[...] = jnp.transpose(jnp.broadcast_to(joined(row_ring), (128, HALF)))
    for k in range(1, RING):
        arrived(col_ring.at[k], scol_send.at[k], scol_recv.at[k], y_peers[k - 1])
    col_stat[...] = joined(col_ring)

    @pl.loop(0, 4)
    def _(n):
        rows = pl.ds(pl.multiple_of(n * 128, 128), 128)
        at_lane = lax.broadcasted_iota(jnp.int32, (1, 2 * HALF), 1)
        member = (at_lane >> 5) & 15
        along, parity = member >> 1, member & 1
        its_core = jnp.where(at_lane < HALF, core, 1 - core)
        its_x = jnp.where(parity == p, x, xb)
        its_blk = (its_x * 4 + (along & 3)) * 2 + its_core
        its_dp = (along >> 2) * 8 + z
        ids = ((its_blk * 16 + its_dp) * R + (at_lane & 31)).astype(F32)
        digit = images[rows, E:].astype(F32)
        label = digit[:, 0:1] * 128.0 + digit[:, 64:65]
        tile = logits[rows, :]
        target = jnp.where(label == ids, 2.0, 0.0)
        both = jnp.exp(tile - row_stat[rows, 0:1]) + jnp.exp(tile - col_stat[...])
        weight = (both - target) * 0.5
        wts[rows, :] = weight.astype(BF16)
        wts_t[:, rows] = jnp.transpose(weight).astype(BF16)

    for n in range(4):
        cols = pl.ds(n * 256, 256)
        swap_out[:, cols] = jnp.dot(
            wts_t[HALF:, :], images[:, cols], preferred_element_type=F32
        ).astype(BF16)
        send(swap_out.at[:, cols], swap_in.at[:, cols], swap_send.at[n], swap_recv.at[n], sibling)

    @pl.loop(0, 4)
    def _(n):
        cols = pl.ds(pl.multiple_of(n * 256, 256), 256)
        grad_i[:, cols] = jnp.dot(wts[...], texts[:, cols], preferred_element_type=F32)

    def own_term(kind, where, q):
        slot = where * 2 + (p if q == 0 else 1 - p)
        return (grad_i if kind == 0 else grad_t)[rows_at(slot), :]

    def pass_on(kind, d, q, s):
        term = own_term(kind, up(place[kind], SIGNS[d] * (hops(d, q) - s)), q)
        if s > 0:
            came = landed.at[kind, d, q, s - 1]
            arrived(came, rs_send.at[kind, d, q, s - 1], rs_recv.at[kind, d, q, s - 1], ahead[kind][d])
            term = term + came[...].astype(F32)
        stage[kind, d, q, s] = term.astype(BF16)
        send(
            stage.at[kind, d, q, s], landed.at[kind, d, q, s],
            rs_send.at[kind, d, q, s], rs_recv.at[kind, d, q, s], ahead[kind][d],
        )

    for d, q in order:
        pass_on(0, d, q, 0)

    @pl.loop(0, 4)
    def _(n):
        cols = pl.ds(pl.multiple_of(n * 256, 256), 256)
        grad_t[:, cols] = jnp.dot(wts_t[:HALF, :], images[:, cols], preferred_element_type=F32)

    for n in range(4):
        cols = pl.ds(n * 256, 256)
        arrived(swap_in.at[:, cols], swap_send.at[n], swap_recv.at[n], sibling)
    grad_t[...] = grad_t[...] + swap_in[...].astype(F32)
    for d, q in order:
        pass_on(1, d, q, 0)
    for s in range(1, 4):
        for kind in range(2):
            for d, q in order:
                if s < hops(d, q):
                    pass_on(kind, d, q, s)

    def complete(kind, q):
        total = own_term(kind, place[kind], q)
        for d in range(2):
            s = hops(d, q) - 1
            came = landed.at[kind, d, q, s]
            arrived(came, rs_send.at[kind, d, q, s], rs_recv.at[kind, d, q, s], ahead[kind][d])
            total = total + came[...].astype(F32)
        return total

    for kind in range(2):
        last_out[kind] = complete(kind, 1).astype(BF16)
        send(last_out.at[kind], last_in.at[kind], last_send.at[kind], last_recv.at[kind], pair[kind])
    for kind, out_ref in ((0, out_image_ref), (1, out_text_ref)):
        total = complete(kind, 0)
        arrived(last_in.at[kind], last_send.at[kind], last_recv.at[kind], pair[kind])
        out_ref[...] = (scale * (total + last_in[kind].astype(F32))).astype(BF16)

    for one in sent:
        one.wait_send()


def per_device(image_emb, text_emb, labels, logit_scale):
    vmem = pl.BlockSpec(memory_space=pltpu.VMEM)
    smem = pl.BlockSpec(memory_space=pltpu.SMEM)
    dma = pltpu.SemaphoreType.DMA
    out = jax.ShapeDtypeStruct((R, E), BF16)
    return pl.pallas_call(
        kernel,
        out_shape=(out, out),
        in_specs=[vmem, vmem, smem, smem],
        out_specs=(vmem, vmem),
        scratch_shapes=[
            pltpu.VMEM((HALF, W), BF16),
            pltpu.VMEM((2 * HALF, E), BF16),
            pltpu.VMEM((HALF, 2 * HALF), F32),
            pltpu.VMEM((HALF, 2 * HALF), BF16),
            pltpu.VMEM((2 * HALF, HALF), BF16),
            pltpu.VMEM((HALF, E), F32),
            pltpu.VMEM((HALF, E), F32),
            pltpu.VMEM((HALF, 128), F32),
            pltpu.VMEM((1, 2 * HALF), F32),
            pltpu.VMEM((1, HALF), F32),
            pltpu.VMEM((1, HALF), F32),
            pltpu.VMEM((RING, 1, HALF), F32),
            pltpu.VMEM((1, 2 * HALF), F32),
            pltpu.VMEM((3, 1, 2 * HALF), F32),
            pltpu.VMEM((RING, 1, 2 * HALF), F32),
            pltpu.VMEM((HALF, E), BF16),
            pltpu.VMEM((HALF, E), BF16),
            pltpu.VMEM((2, 2, 2, 4, R, E), BF16),
            pltpu.VMEM((2, 2, 2, 4, R, E), BF16),
            pltpu.VMEM((2, R, E), BF16),
            pltpu.VMEM((2, R, E), BF16),
            dma((2,)), dma((2,)),
            dma((2, 2, 2, 4)), dma((2, 2, 2, 4)),
            dma((2, RING)), dma((2, RING)),
            dma((4,)), dma((4,)),
            dma((RING,)), dma((RING,)),
            dma((RING,)), dma((RING,)),
            dma((4,)), dma((4,)),
            dma((2, 2, 2, 4)), dma((2, 2, 2, 4)),
            dma((2,)), dma((2,)),
        ],
        compiler_params=pltpu.CompilerParams(
            collective_id=0, has_side_effects=True, vmem_limit_bytes=40 * 1024 * 1024
        ),
        cost_estimate=pl.CostEstimate(flops=3221225472, bytes_accessed=262144, transcendentals=2097152),
        name="contrastive",
    )(image_emb, text_emb, labels, logit_scale.reshape(1))


def solution(mesh):
    in_specs = (P(("blk", "dp"), None), P(("blk", "dp"), None), P(("blk", "dp")), P())
    out_specs = (P(("blk", "dp"), None), P(("blk", "dp"), None))
    return jax.shard_map(
        per_device, mesh=mesh, in_specs=in_specs, out_specs=out_specs, check_vma=False
    )
```

time: 718 us -> 80.6 us (0.11)
  the two profiles are of different devices: /device:TPU:1 before, /device:TPU:8 now
where the time goes in v1:
time: 80.6 us; the launch traced here: 80.4 us
  Pallas kernels  75.5 us (94%)
  local copies, waits for them, and re-layouts  3.59 us (4%)
  between operations  1.3 us (2%)
    pallas_call x1, Pallas kernels, per_device(): pl.pallas_call(kernel, out_shape=(out, out), in_specs=[vmem, vmem, smem,...  75.5 us
    unnamed x8, local copies, waits for them, and re-layouts  3.59 us

profile of v1, /device:TPU:8, one launch (start us, length us, event | category | flops | bytes accessed | tf_op | source)
XLA Modules:
  0.0 80.4 jit_solution(6934785550026667304)
XLA Ops:
  1.3 0.0 copy-start.2
  1.3 0.6 copy-done.2
  1.9 0.0 copy-start
  1.9 0.8 %copy-done = bf16[32,1024]{1,0:T(8,128)(2,1)S(1)} copy-done((bf16[32,1024]{1,0:T(8,128)(2,1)S(1)}, bf16[32,1024]{1,0:T(8,128)(2,1)}, u32[]{:S(2)}) %copy-start) | copy-done | bytes 65560
  2.8 0.0 copy-start.1
  2.8 0.8 %copy-done.1 = bf16[32,1024]{1,0:T(8,128)(2,1)S(1)} copy-done((bf16[32,1024]{1,0:T(8,128)(2,1)S(1)}, bf16[32,1024]{1,0:T(8,128)(2,1)}, u32[]{:S(2)}) %copy-start.1) | copy-done | bytes 65560
  3.6 75.5 %contrastive.1 = (bf16[32,1024]{1,0:T(8,128)(2,1)S(1)}, bf16[32,1024]{1,0:T(8,128)(2,1)S(1)}) custom-call(bf16[32,1024]{1,0:T(8,128)(2,1)S(1)} %copy-done, bf16[32,1024]{1,0:T(8,128)(2,1)S(1)} %copy-done.1, s32[32]{0:T(128)S(1)} %copy-done.2, f32[1]{0:T(128)} %bitcast.1.scale_ref), custom_call_target="tpu_custom_call" | custom-call | flops 3221225472 | bytes 262144 | tf_op jit(solution)/shard_map/contrastive/pallas_call | solution.py:294
  79.1 0.6 copy.9
  79.8 0.6 copy.10
Async XLA Ops:
  1.3 0.7 copy-start.2
  1.9 0.8 %copy-start = (bf16[32,1024]{1,0:T(8,128)(2,1)S(1)}, bf16[32,1024]{1,0:T(8,128)(2,1)}, u32[]{:S(2)}) copy-start(bf16[32,1024]{1,0:T(8,128)(2,1)} %image_ref.1) | copy-start | bytes 196612
  2.8 0.8 %copy-start.1 = (bf16[32,1024]{1,0:T(8,128)(2,1)S(1)}, bf16[32,1024]{1,0:T(8,128)(2,1)}, u32[]{:S(2)}) copy-start(bf16[32,1024]{1,0:T(8,128)(2,1)} %text_ref.1) | copy-start | bytes 196612

commit v2 on v1

v2 whole, which is shorter than its diff:
```python
import jax
import jax.numpy as jnp
from jax import lax
from jax.experimental import pallas as pl
from jax.experimental.pallas import tpu as pltpu
from jax.sharding import PartitionSpec as P

R = 32
H = R // 2
E = 1024
W = E + 128
RING = 8
HALF = RING * 2 * R
GROUP = 2 * RING
F32 = jnp.float32
BF16 = jnp.bfloat16
MESH = pl.DeviceIdType.MESH

STAGES = (
    ((1, 0, 0), (0, 1, 2), (0, 1, -2), (0, 0, 1), (0, 0, -1), (0, 1, 1), (0, 1, -1), (1, 1, 0)),
    (
        (1, 0, 2), (1, 0, -2), (0, 1, 4), (0, 1, 3), (0, 1, -3), (0, 0, 2), (0, 0, -2),
        (1, 0, 1), (1, 0, -1), (1, 1, 2), (1, 1, -2), (1, 1, 1), (1, 1, -1),
    ),
    (
        (0, 0, 4), (0, 0, 3), (0, 0, -3), (1, 0, 4), (1, 0, 3), (1, 0, -3),
        (1, 1, 4), (1, 1, 3), (1, 1, -3),
    ),
)


def parent(piece):
    q, h, d = piece
    if q == 1 and (h == 1 or d == 0):
        return (0, h, d), 0
    if d == 4:
        step = -2 if (q, h) == (0, 1) else 2
        return (q, h, step), step
    step = d if abs(d) == 2 and q != h else (1 if d > 0 else -1)
    return (q, h, d - step), step


CHILDREN = {}
for _stage in STAGES:
    for _piece in _stage:
        CHILDREN.setdefault(parent(_piece)[0], []).append(_piece)
BACKWARDS = [_piece for _stage in STAGES[::-1] for _piece in _stage]


def lse2(a, b):
    top = jnp.maximum(a, b)
    return top + jnp.log(jnp.exp(a - top) + jnp.exp(b - top))


def kernel(
    image_ref, text_ref, label_ref, scale_ref, out_image_ref, out_text_ref,
    images, texts, logits, wts, wts_t, grad_i, grad_t, row_stat, col_stat,
    row_ring, col_vec, col_sib, col_ring, labels,
    swap_out, swap_in, stage, landed,
    load_sem, ring_send, ring_recv, sib_send, sib_recv, stat_send, stat_recv,
    srow_send, srow_recv, scol_send, scol_recv, swap_send, swap_recv, rs_send, rs_recv,
):
    blk, dp = lax.axis_index("blk"), lax.axis_index("dp")
    core, x = blk % 2, blk // 8
    y, z = (dp // 8) * 4 + (blk // 2) % 4, dp % 8
    p = x % 2
    xa = x + 1 - 2 * p
    xb = (x + 2 * p + 3) % 4
    sense = 1 - 2 * core

    def at(x=x, y=y, z=z, core=core):
        return {"blk": (x * 4 + y % 4) * 2 + core, "dp": (y // 4) * 8 + z}

    def along(v, d):
        return (v + sense * d + RING) % RING

    sibling = at(core=1 - core)
    image_peers = [at(x=x if q == 0 else xa, z=along(z, k)) for q in range(2) for k in range(RING)]
    text_peers = [at(x=x if q == 0 else xb, y=along(y, k)) for q in range(2) for k in range(RING)]

    own_image = pl.ds(pl.multiple_of((z * 2 + p) * R, R), R)
    own_text = pl.ds(pl.multiple_of((y * 2 + p) * R, R), R)
    loads = [
        pltpu.make_async_copy(label_ref, labels, load_sem.at[0]),
        pltpu.make_async_copy(image_ref, images.at[own_image, pl.ds(0, E)], load_sem.at[1]),
        pltpu.make_async_copy(text_ref, texts.at[own_text], load_sem.at[2]),
    ]
    for load in loads:
        load.start()
    barrier = pltpu.get_barrier_semaphore()
    steps = (1, RING - 1, 2, RING - 2, RING)
    peers = [sibling] + [image_peers[k] for k in steps] + [text_peers[k] for k in steps]
    for peer in peers:
        pl.semaphore_signal(barrier, inc=1, device_id=peer, device_id_type=MESH)
    loads[0].wait()
    digits = jnp.zeros((R, 128), jnp.int32)
    row_of = lax.broadcasted_iota(jnp.int32, (R, 128), 0)
    for r in range(R):
        digits = jnp.where(row_of == r, labels[r], digits)
    lane = lax.broadcasted_iota(jnp.int32, (R, 128), 1)
    digits = jnp.where(lane < 64, digits >> 7, digits & 127)
    images[own_image, E:] = digits.astype(F32).astype(BF16)
    loads[1].wait()
    loads[2].wait()
    pl.semaphore_wait(barrier, len(peers))

    sent = []

    def copy(src, dst, ssem, rsem, peer):
        return pltpu.make_async_remote_copy(
            src_ref=src, dst_ref=dst, send_sem=ssem, recv_sem=rsem, device_id=peer, device_id_type=MESH
        )

    def send(src, dst, ssem, rsem, peer):
        one = copy(src, dst, ssem, rsem, peer)
        one.start()
        sent.append(one)

    def arrived(dst, ssem, rsem, peer):
        copy(dst, dst, ssem, rsem, peer).wait_recv()

    place = (z, y)

    def peer_of(kind, step):
        if step == 0:
            return at(x=xa) if kind == 0 else at(x=xb)
        return at(z=along(z, step)) if kind == 0 else at(y=along(y, step))

    def piece_rows(kind, piece):
        q, h, d = piece
        slot = along(place[kind], -d) * 2 + (p if q == 0 else 1 - p)
        return pl.ds(pl.multiple_of(slot * R + h * H, H), H)

    def held(kind, piece):
        return (images if kind == 0 else texts).at[piece_rows(kind, piece)]

    def index(kind, piece):
        q, h, d = piece
        return kind, q, h, d + 3

    def gather_send(kind, piece):
        source, step = parent(piece)
        part, i = held(kind, source), index(kind, piece)
        send(part, part, ring_send.at[i], ring_recv.at[i], peer_of(kind, step))

    def sibling_rows(q, d):
        slot = along(y, -d) * 2 + (p if q == 0 else 1 - p)
        return pl.ds(pl.multiple_of(slot * R, R), R), pl.ds(pl.multiple_of(slot * R + HALF, R), R)

    def theirs(q, d):
        return sibling_rows(q, d)[1], (q, d + 3)

    def to_sibling(q, d):
        mine, there = sibling_rows(q, d)
        i = (q, (d if d == 4 else -d) + 3)
        send(texts.at[mine], texts.at[there], sib_send.at[i], sib_recv.at[i], sibling)

    for piece in STAGES[0]:
        for kind in range(2):
            gather_send(kind, piece)
    to_sibling(0, 0)
    got = set()
    for pieces in STAGES:
        for piece in pieces:
            q, h, d = piece
            for kind in (1, 0):
                i = index(kind, piece)
                arrived(held(kind, piece), ring_send.at[i], ring_recv.at[i], peer_of(kind, 0))
                for child in CHILDREN.get(piece, ()):
                    gather_send(kind, child)
            got.add(piece)
            if (q, 0, d) in got and (q, 1, d) in got:
                to_sibling(q, d)

    scale = scale_ref[0]

    def logits_of(n):
        cols = pl.ds(pl.multiple_of(n * 256, 256), 256)
        tile = scale * lax.dot_general(
            images[:, :E], texts[cols, :], (((1,), (1,)), ((), ())), preferred_element_type=F32
        )
        logits[:, cols] = tile
        top = jnp.max(tile, axis=0, keepdims=True)
        total = jnp.sum(jnp.exp(tile - top), axis=0, keepdims=True)
        col_vec[:, cols] = top + jnp.log(total)

    pl.loop(0, 2)(logits_of)
    for q in range(2):
        for d in range(-3, 5):
            rows, i = theirs(q, d)
            arrived(texts.at[rows], sib_send.at[i], sib_recv.at[i], sibling)
    pl.loop(2, 4)(logits_of)
    send(col_vec, col_sib, stat_send, stat_recv, sibling)

    @pl.loop(0, 8)
    def _(n):
        rows = pl.ds(pl.multiple_of(n * 64, 64), 64)
        tile = logits[rows, :]
        top = jnp.max(tile, axis=1, keepdims=True)
        total = jnp.sum(jnp.exp(tile - top), axis=1, keepdims=True)
        row_stat[rows, :] = jnp.broadcast_to(top + jnp.log(total), (64, 128))

    row_ring[0] = jnp.transpose(row_stat[...])[0:1, :]

    for k in range(1, GROUP):
        send(row_ring.at[0], row_ring.at[k], srow_send.at[k], srow_recv.at[k], image_peers[k])
    arrived(col_sib, stat_send, stat_recv, sibling)
    from_sibling = col_sib[...]
    from_sibling = jnp.concatenate([from_sibling[:, HALF:], from_sibling[:, :HALF]], axis=1)
    col_ring[0] = lse2(col_vec[...], from_sibling)
    for k in range(1, GROUP):
        send(col_ring.at[0], col_ring.at[k], scol_send.at[k], scol_recv.at[k], text_peers[k])
    for k in range(1, GROUP):
        arrived(row_ring.at[k], srow_send.at[k], srow_recv.at[k], image_peers[k])

    def joined(ring):
        parts = [ring[k] for k in range(GROUP)]
        top = parts[0]
        for part in parts[1:]:
            top = jnp.maximum(top, part)
        total = jnp.exp(parts[0] - top)
        for part in parts[1:]:
            total = total + jnp.exp(part - top)
        return top + jnp.log(total)

    row_stat[...] = jnp.transpose(jnp.broadcast_to(joined(row_ring), (128, HALF)))
    for k in range(1, GROUP):
        arrived(col_ring.at[k], scol_send.at[k], scol_recv.at[k], text_peers[k])
    col_stat[...] = joined(col_ring)

    @pl.loop(0, 4)
    def _(n):
        rows = pl.ds(pl.multiple_of(n * 128, 128), 128)
        at_lane = lax.broadcasted_iota(jnp.int32, (1, 2 * HALF), 1)
        member = (at_lane >> 5) & 15
        its_y, parity = member >> 1, member & 1
        its_core = jnp.where(at_lane < HALF, core, 1 - core)
        its_x = jnp.where(parity == p, x, xb)
        its_blk = (its_x * 4 + (its_y & 3)) * 2 + its_core
        its_dp = (its_y >> 2) * 8 + z
        ids = ((its_blk * 16 + its_dp) * R + (at_lane & 31)).astype(F32)
        digit = images[rows, E:].astype(F32)
        label = digit[:, 0:1] * 128.0 + digit[:, 64:65]
        tile = logits[rows, :]
        target = jnp.where(label == ids, 2.0, 0.0)
        both = jnp.exp(tile - row_stat[rows, 0:1]) + jnp.exp(tile - col_stat[...])
        weight = (both - target) * 0.5
        wts[rows, :] = weight.astype(BF16)
        wts_t[:, rows] = jnp.transpose(weight).astype(BF16)

    for n in range(4):
        cols = pl.ds(n * 256, 256)
        swap_out[:, cols] = jnp.dot(
            wts_t[HALF:, :], images[:, cols], preferred_element_type=F32
        ).astype(BF16)
        send(swap_out.at[:, cols], swap_in.at[:, cols], swap_send.at[n], swap_recv.at[n], sibling)

    def summed(kind, piece):
        total = (grad_i if kind == 0 else grad_t)[piece_rows(kind, piece), :]
        for child in CHILDREN.get(piece, ()):
            i = index(kind, child)
            arrived(landed.at[i], rs_send.at[i], rs_recv.at[i], peer_of(kind, 0))
            total = total + landed[i].astype(F32)
        return total

    def pass_on(kind, piece):
        i = index(kind, piece)
        stage[i] = summed(kind, piece).astype(BF16)
        send(stage.at[i], landed.at[i], rs_send.at[i], rs_recv.at[i], peer_of(kind, -parent(piece)[1]))

    leaves = [piece for piece in BACKWARDS if piece not in CHILDREN]

    @pl.loop(0, 4)
    def _(n):
        cols = pl.ds(pl.multiple_of(n * 256, 256), 256)
        grad_i[:, cols] = jnp.dot(wts[...], texts[:, cols], preferred_element_type=F32)

    for piece in leaves:
        pass_on(0, piece)

    @pl.loop(0, 4)
    def _(n):
        cols = pl.ds(pl.multiple_of(n * 256, 256), 256)
        grad_t[:, cols] = jnp.dot(wts_t[:HALF, :], images[:, cols], preferred_element_type=F32)

    for n in range(4):
        cols = pl.ds(n * 256, 256)
        arrived(swap_in.at[:, cols], swap_send.at[n], swap_recv.at[n], sibling)
    grad_t[...] = grad_t[...] + swap_in[...].astype(F32)
    for piece in leaves:
        pass_on(1, piece)
    for piece in BACKWARDS:
        if piece in CHILDREN:
            for kind in range(2):
                pass_on(kind, piece)
    for kind, out_ref in ((0, out_image_ref), (1, out_text_ref)):
        for h in range(2):
            out_ref[pl.ds(h * H, H), :] = (scale * summed(kind, (0, h, 0))).astype(BF16)

    for one in sent:
        one.wait_send()


def per_device(image_emb, text_emb, labels, logit_scale):
    vmem = pl.BlockSpec(memory_space=pltpu.VMEM)
    smem = pl.BlockSpec(memory_space=pltpu.SMEM)
    hbm = pl.BlockSpec(memory_space=pltpu.HBM)
    dma = pltpu.SemaphoreType.DMA
    out = jax.ShapeDtypeStruct((R, E), BF16)
    return pl.pallas_call(
        kernel,
        out_shape=(out, out),
        in_specs=[hbm, hbm, hbm, smem],
        out_specs=(vmem, vmem),
        scratch_shapes=[
            pltpu.VMEM((HALF, W), BF16),
            pltpu.VMEM((2 * HALF, E), BF16),
            pltpu.VMEM((HALF, 2 * HALF), F32),
            pltpu.VMEM((HALF, 2 * HALF), BF16),
            pltpu.VMEM((2 * HALF, HALF), BF16),
            pltpu.VMEM((HALF, E), F32),
            pltpu.VMEM((HALF, E), F32),
            pltpu.VMEM((HALF, 128), F32),
            pltpu.VMEM((1, 2 * HALF), F32),
            pltpu.VMEM((GROUP, 1, HALF), F32),
            pltpu.VMEM((1, 2 * HALF), F32),
            pltpu.VMEM((1, 2 * HALF), F32),
            pltpu.VMEM((GROUP, 1, 2 * HALF), F32),
            pltpu.SMEM((R,), jnp.int32),
            pltpu.VMEM((HALF, E), BF16),
            pltpu.VMEM((HALF, E), BF16),
            pltpu.VMEM((2, 2, 2, RING, H, E), BF16),
            pltpu.VMEM((2, 2, 2, RING, H, E), BF16),
            dma((3,)),
            dma((2, 2, 2, RING)), dma((2, 2, 2, RING)),
            dma((2, RING)), dma((2, RING)),
            dma(()), dma(()),
            dma((GROUP,)), dma((GROUP,)),
            dma((GROUP,)), dma((GROUP,)),
            dma((4,)), dma((4,)),
            dma((2, 2, 2, RING)), dma((2, 2, 2, RING)),
        ],
        compiler_params=pltpu.CompilerParams(
            collective_id=0, has_side_effects=True, vmem_limit_bytes=40 * 1024 * 1024
        ),
        cost_estimate=pl.CostEstimate(flops=3221225472, bytes_accessed=262144, transcendentals=2097152),
        name="contrastive",
    )(image_emb, text_emb, labels, logit_scale.reshape(1))


def solution(mesh):
    in_specs = (P(("blk", "dp"), None), P(("blk", "dp"), None), P(("blk", "dp")), P())
    out_specs = (P(("blk", "dp"), None), P(("blk", "dp"), None))
    return jax.shard_map(
        per_device, mesh=mesh, in_specs=in_specs, out_specs=out_specs, check_vma=False
    )
```

time: 80.6 us -> 70.1 us (0.87)
  the two profiles are of different devices: /device:TPU:8 before, /device:TPU:1 now
where the time goes in v2:
time: 70.1 us; the launch traced here: 69.5 us
  Pallas kernels  64.6 us (92%)
  local copies, waits for them, and re-layouts  3.59 us (5%)
  between operations  1.3 us (2%)
    pallas_call x1, Pallas kernels, per_device(): pl.pallas_call(kernel, out_shape=(out, out), in_specs=[hbm, hbm, hbm, sme...  64.6 us
    unnamed x8, local copies, waits for them, and re-layouts  3.59 us

profile of v2, /device:TPU:1, one launch (start us, length us, event | category | flops | bytes accessed | tf_op | source)
XLA Modules:
  0.0 69.5 jit_solution(8635088046241052759)
XLA Ops:
  1.3 0.0 copy-start.2
  1.3 0.6 copy-done.2
  1.9 0.0 copy-start
  1.9 0.8 %copy-done = bf16[32,1024]{1,0:T(8,128)(2,1)S(1)} copy-done((bf16[32,1024]{1,0:T(8,128)(2,1)S(1)}, bf16[32,1024]{1,0:T(8,128)(2,1)}, u32[]{:S(2)}) %copy-start) | copy-done | bytes 65560
  2.8 0.0 copy-start.1
  2.8 0.8 %copy-done.1 = bf16[32,1024]{1,0:T(8,128)(2,1)S(1)} copy-done((bf16[32,1024]{1,0:T(8,128)(2,1)S(1)}, bf16[32,1024]{1,0:T(8,128)(2,1)}, u32[]{:S(2)}) %copy-start.1) | copy-done | bytes 65560
  3.6 64.6 %contrastive.1 = (bf16[32,1024]{1,0:T(8,128)(2,1)S(1)}, bf16[32,1024]{1,0:T(8,128)(2,1)S(1)}) custom-call(bf16[32,1024]{1,0:T(8,128)(2,1)S(1)} %copy-done, bf16[32,1024]{1,0:T(8,128)(2,1)S(1)} %copy-done.1, s32[32]{0:T(128)S(1)} %copy-done.2, f32[1]{0:T(128)} %bitcast.1.scale_ref), custom_call_target="tpu_custom_call" | custom-call | flops 3221225472 | bytes 262144 | tf_op jit(solution)/shard_map/contrastive/pallas_call | solution.py:310
  68.2 0.6 copy.9
  68.9 0.6 copy.10
Async XLA Ops:
  1.3 0.7 copy-start.2
  1.9 0.8 %copy-start = (bf16[32,1024]{1,0:T(8,128)(2,1)S(1)}, bf16[32,1024]{1,0:T(8,128)(2,1)}, u32[]{:S(2)}) copy-start(bf16[32,1024]{1,0:T(8,128)(2,1)} %image_ref.1) | copy-start | bytes 196612
  2.8 0.8 %copy-start.1 = (bf16[32,1024]{1,0:T(8,128)(2,1)S(1)}, bf16[32,1024]{1,0:T(8,128)(2,1)}, u32[]{:S(2)}) copy-start(bf16[32,1024]{1,0:T(8,128)(2,1)} %text_ref.1) | copy-start | bytes 196612

commit v3 on v2

v3 whole, which is shorter than its diff:
```python
import jax
import jax.numpy as jnp
from jax import lax
from jax.experimental import pallas as pl
from jax.experimental.pallas import tpu as pltpu
from jax.sharding import PartitionSpec as P

R = 32
H = R // 2
E = 1024
RING = 8
HALF = RING * 2 * R
GROUP = 2 * RING
F32 = jnp.float32
BF16 = jnp.bfloat16
MESH = pl.DeviceIdType.MESH

STAGES = (
    ((1, 0, 0), (0, 1, 2), (0, 1, -2), (0, 0, 1), (0, 0, -1), (0, 1, 1), (0, 1, -1), (1, 1, 0)),
    (
        (1, 0, 2), (1, 0, -2), (0, 1, 4), (0, 1, 3), (0, 1, -3), (0, 0, 2), (0, 0, -2),
        (1, 0, 1), (1, 0, -1), (1, 1, 2), (1, 1, -2), (1, 1, 1), (1, 1, -1),
    ),
    (
        (0, 0, 4), (0, 0, 3), (0, 0, -3), (1, 0, 4), (1, 0, 3), (1, 0, -3),
        (1, 1, 4), (1, 1, 3), (1, 1, -3),
    ),
)


def parent(piece):
    q, h, d = piece
    if q == 1 and (h == 1 or d == 0):
        return (0, h, d), 0
    if d == 4:
        step = -2 if (q, h) == (0, 1) else 2
        return (q, h, step), step
    step = d if abs(d) == 2 and q != h else (1 if d > 0 else -1)
    return (q, h, d - step), step


CHILDREN = {}
for _stage in STAGES:
    for _piece in _stage:
        CHILDREN.setdefault(parent(_piece)[0], []).append(_piece)
BACKWARDS = [_piece for _stage in STAGES[::-1] for _piece in _stage]


def lse2(a, b):
    top = jnp.maximum(a, b)
    return top + jnp.log(jnp.exp(a - top) + jnp.exp(b - top))


def kernel(
    image_ref, text_ref, label_ref, scale_ref, out_image_ref, out_text_ref,
    images, texts, logits, wts, wts_t, grad_i, grad_t, row_stat, col_stat,
    row_ring, col_vec, col_sib, col_ring, label_stat, labels,
    swap_out, swap_in, grad_i16, grad_t16, stage, landed,
    load_sem, ring_send, ring_recv, sib_send, sib_recv, stat_send, stat_recv,
    srow_send, srow_recv, scol_send, scol_recv, swap_send, swap_recv, rs_send, rs_recv,
):
    blk, dp = lax.axis_index("blk"), lax.axis_index("dp")
    core, x = blk % 2, blk // 8
    y, z = (dp // 8) * 4 + (blk // 2) % 4, dp % 8
    p = x % 2
    xa = x + 1 - 2 * p
    xb = (x + 2 * p + 3) % 4
    sense = 1 - 2 * core

    def at(x=x, y=y, z=z, core=core):
        return {"blk": (x * 4 + y % 4) * 2 + core, "dp": (y // 4) * 8 + z}

    def along(v, d):
        return (v + sense * d + RING) % RING

    sibling = at(core=1 - core)
    image_peers = [at(x=x if q == 0 else xa, z=along(z, k)) for q in range(2) for k in range(RING)]
    text_peers = [at(x=x if q == 0 else xb, y=along(y, k)) for q in range(2) for k in range(RING)]

    own_image = pl.ds(pl.multiple_of((z * 2 + p) * R, R), R)
    own_text = pl.ds(pl.multiple_of((y * 2 + p) * R, R), R)
    loads = [
        pltpu.make_async_copy(label_ref, labels, load_sem.at[0]),
        pltpu.make_async_copy(image_ref, images.at[own_image], load_sem.at[1]),
        pltpu.make_async_copy(text_ref, texts.at[own_text], load_sem.at[2]),
    ]
    for load in loads:
        load.start()
    barrier = pltpu.get_barrier_semaphore()
    steps = (1, RING - 1, 2, RING - 2, RING)
    peers = [sibling] + [image_peers[k] for k in steps] + [text_peers[k] for k in steps]
    for peer in peers:
        pl.semaphore_signal(barrier, inc=1, device_id=peer, device_id_type=MESH)
    loads[1].wait()
    loads[2].wait()
    loads[0].wait()
    pl.semaphore_wait(barrier, len(peers))

    def copy(src, dst, ssem, rsem, peer):
        return pltpu.make_async_remote_copy(
            src_ref=src, dst_ref=dst, send_sem=ssem, recv_sem=rsem, device_id=peer, device_id_type=MESH
        )

    def send(src, dst, ssem, rsem, peer):
        copy(src, dst, ssem, rsem, peer).start()

    def arrived(dst, ssem, rsem):
        copy(dst, dst, ssem, rsem, sibling).wait_recv()

    def left(src, ssem, rsem):
        copy(src, src, ssem, rsem, sibling).wait_send()

    place = (z, y)

    def peer_of(kind, step):
        if step == 0:
            return at(x=xa) if kind == 0 else at(x=xb)
        return at(z=along(z, step)) if kind == 0 else at(y=along(y, step))

    def piece_rows(kind, piece):
        q, h, d = piece
        slot = along(place[kind], -d) * 2 + (p if q == 0 else 1 - p)
        return pl.ds(pl.multiple_of(slot * R + h * H, H), H)

    def held(kind, piece):
        return (images if kind == 0 else texts).at[piece_rows(kind, piece)]

    def index(kind, piece):
        q, h, d = piece
        return kind, q, h, d + 3

    def gather_send(kind, piece):
        source, step = parent(piece)
        part, i = held(kind, source), index(kind, piece)
        send(part, part, ring_send.at[kind], ring_recv.at[i], peer_of(kind, step))

    def to_sibling(d):
        slot = along(y, -d) * 2
        mine = pl.ds(pl.multiple_of(slot * R, 2 * R), 2 * R)
        there = pl.ds(pl.multiple_of(slot * R + HALF, 2 * R), 2 * R)
        send(texts.at[mine], texts.at[there], sib_send, sib_recv, sibling)

    for piece in STAGES[0]:
        for kind in range(2):
            gather_send(kind, piece)
    got = {(0, 0, 0), (0, 1, 0)}
    for pieces in STAGES:
        for piece in pieces:
            d = piece[2]
            for kind in (1, 0):
                i = index(kind, piece)
                arrived(held(kind, piece), ring_send.at[kind], ring_recv.at[i])
                for child in CHILDREN.get(piece, ()):
                    gather_send(kind, child)
                got.add(piece)
                if kind == 1 and all((q, h, d) in got for q in range(2) for h in range(2)):
                    to_sibling(d)

    scale = scale_ref[0]

    @pl.loop(0, 4)
    def _(n):
        @pl.when(n == 2)
        def _():
            arrived(texts.at[pl.ds(HALF, HALF)], sib_send, sib_recv)

        cols = pl.ds(pl.multiple_of(n * 256, 256), 256)
        tile = scale * lax.dot_general(
            images[...], texts[cols, :], (((1,), (1,)), ((), ())), preferred_element_type=F32
        )
        logits[:, cols] = tile
        top = jnp.max(tile, axis=0, keepdims=True)
        total = jnp.sum(jnp.exp(tile - top), axis=0, keepdims=True)
        col_vec[:, cols] = top + jnp.log(total)

    send(col_vec, col_sib, stat_send, stat_recv, sibling)

    at_label = lax.broadcasted_iota(jnp.int32, (1, HALF), 1) - (z * 2 + p) * R
    own_labels = jnp.zeros((1, HALF), jnp.int32)
    for r in range(R):
        own_labels = jnp.where(at_label == r, labels[r], own_labels)
    row_ring[0, 1:2, :] = own_labels.astype(F32)

    @pl.loop(0, 4)
    def _(n):
        @pl.when(n == 2)
        def _():
            arrived(col_sib, stat_send, stat_recv)
            from_sibling = col_sib[...]
            from_sibling = jnp.concatenate([from_sibling[:, HALF:], from_sibling[:, :HALF]], axis=1)
            col_ring[0] = lse2(col_vec[...], from_sibling)
            for k in range(1, GROUP):
                send(col_ring.at[0], col_ring.at[k], scol_send, scol_recv, text_peers[k])

        rows = pl.ds(pl.multiple_of(n * 128, 128), 128)
        tile = logits[rows, :]
        top = jnp.max(tile, axis=1, keepdims=True)
        total = jnp.sum(jnp.exp(tile - top), axis=1, keepdims=True)
        row_stat[rows, :] = jnp.broadcast_to(top + jnp.log(total), (128, 128))

    row_ring[0, 0:1, :] = jnp.transpose(row_stat[...])[0:1, :]
    for k in range(1, GROUP):
        send(row_ring.at[0], row_ring.at[k], srow_send, srow_recv, image_peers[k])

    gathered = pl.ds(0, HALF - R)
    left(images.at[gathered], ring_send.at[0], sib_recv)
    left(texts.at[gathered], ring_send.at[1], sib_recv)
    left(texts.at[pl.ds(0, HALF)], sib_send, sib_recv)
    left(col_vec, stat_send, stat_recv)

    def joined(ring):
        parts = [ring[k, 0:1, :] for k in range(GROUP)]
        top = parts[0]
        for part in parts[1:]:
            top = jnp.maximum(top, part)
        total = jnp.exp(parts[0] - top)
        for part in parts[1:]:
            total = total + jnp.exp(part - top)
        return top + jnp.log(total)

    others = pl.ds(1, GROUP - 1)
    arrived(col_ring.at[others], scol_send, scol_recv)
    col_stat[...] = joined(col_ring)
    arrived(row_ring.at[others], srow_send, srow_recv)
    row_stat[...] = jnp.transpose(jnp.broadcast_to(joined(row_ring), (128, HALF)))
    group_labels = row_ring[0, 1:2, :]
    for k in range(1, GROUP):
        group_labels = group_labels + row_ring[k, 1:2, :]
    label_stat[...] = jnp.transpose(jnp.broadcast_to(group_labels, (128, HALF)))
    left(col_ring.at[others], scol_send, scol_recv)
    left(row_ring.at[others], srow_send, srow_recv)

    @pl.loop(0, 4)
    def _(n):
        rows = pl.ds(pl.multiple_of(n * 128, 128), 128)
        at_lane = lax.broadcasted_iota(jnp.int32, (1, 2 * HALF), 1)
        member = (at_lane >> 5) & 15
        its_y, parity = member >> 1, member & 1
        its_core = jnp.where(at_lane < HALF, core, 1 - core)
        its_x = jnp.where(parity == p, x, xb)
        its_blk = (its_x * 4 + (its_y & 3)) * 2 + its_core
        its_dp = (its_y >> 2) * 8 + z
        ids = ((its_blk * 16 + its_dp) * R + (at_lane & 31)).astype(F32)
        tile = logits[rows, :]
        target = jnp.where(label_stat[rows, 0:1] == ids, 2.0, 0.0)
        both = jnp.exp(tile - row_stat[rows, 0:1]) + jnp.exp(tile - col_stat[...])
        weight = (both - target) * 0.5
        wts[rows, :] = weight.astype(BF16)
        wts_t[:, rows] = jnp.transpose(weight).astype(BF16)

    @pl.loop(0, 4)
    def _(n):
        cols = pl.ds(pl.multiple_of(n * 256, 256), 256)
        swap_out[:, cols] = jnp.dot(
            wts_t[HALF:, :], images[:, cols], preferred_element_type=F32
        ).astype(BF16)
        send(swap_out.at[:, cols], swap_in.at[:, cols], swap_send, swap_recv, sibling)

    def summed(kind, piece):
        total = (grad_i if kind == 0 else grad_t)[piece_rows(kind, piece), :]
        for child in CHILDREN.get(piece, ()):
            i = index(kind, child)
            arrived(landed.at[i], rs_send.at[kind], rs_recv.at[i])
            total = total + landed[i].astype(F32)
        return total

    def pass_on(kind, piece):
        i = index(kind, piece)
        if piece in CHILDREN:
            out = stage.at[i]
            out[...] = summed(kind, piece).astype(BF16)
        else:
            out = (grad_i16 if kind == 0 else grad_t16).at[piece_rows(kind, piece)]
        send(out, landed.at[i], rs_send.at[kind], rs_recv.at[i], peer_of(kind, -parent(piece)[1]))

    leaves = [piece for piece in BACKWARDS if piece not in CHILDREN]

    @pl.loop(0, 4)
    def _(n):
        cols = pl.ds(pl.multiple_of(n * 256, 256), 256)
        term = jnp.dot(wts[...], texts[:, cols], preferred_element_type=F32)
        grad_i[:, cols] = term
        grad_i16[:, cols] = term.astype(BF16)

    for piece in leaves:
        pass_on(0, piece)

    @pl.loop(0, 4)
    def _(n):
        cols = pl.ds(pl.multiple_of(n * 256, 256), 256)
        grad_t[:, cols] = jnp.dot(wts_t[:HALF, :], images[:, cols], preferred_element_type=F32)

    arrived(swap_in, swap_send, swap_recv)

    @pl.loop(0, 8)
    def _(n):
        rows = pl.ds(pl.multiple_of(n * 64, 64), 64)
        term = grad_t[rows, :] + swap_in[rows, :].astype(F32)
        grad_t[rows, :] = term
        grad_t16[rows, :] = term.astype(BF16)

    for piece in leaves:
        pass_on(1, piece)
    for piece in BACKWARDS:
        if piece in CHILDREN:
            for kind in range(2):
                pass_on(kind, piece)
    for kind, out_ref in ((0, out_image_ref), (1, out_text_ref)):
        for h in range(2):
            out_ref[pl.ds(h * H, H), :] = (scale * summed(kind, (0, h, 0))).astype(BF16)

    left(swap_out, swap_send, swap_recv)
    left(grad_i16.at[gathered], rs_send.at[0], swap_recv)
    left(grad_t16.at[gathered], rs_send.at[1], swap_recv)


def per_device(image_emb, text_emb, labels, logit_scale):
    vmem = pl.BlockSpec(memory_space=pltpu.VMEM)
    smem = pl.BlockSpec(memory_space=pltpu.SMEM)
    hbm = pl.BlockSpec(memory_space=pltpu.HBM)
    dma = pltpu.SemaphoreType.DMA
    out = jax.ShapeDtypeStruct((R, E), BF16)
    return pl.pallas_call(
        kernel,
        out_shape=(out, out),
        in_specs=[hbm, hbm, hbm, smem],
        out_specs=(vmem, vmem),
        scratch_shapes=[
            pltpu.VMEM((HALF, E), BF16),
            pltpu.VMEM((2 * HALF, E), BF16),
            pltpu.VMEM((HALF, 2 * HALF), F32),
            pltpu.VMEM((HALF, 2 * HALF), BF16),
            pltpu.VMEM((2 * HALF, HALF), BF16),
            pltpu.VMEM((HALF, E), F32),
            pltpu.VMEM((HALF, E), F32),
            pltpu.VMEM((HALF, 128), F32),
            pltpu.VMEM((1, 2 * HALF), F32),
            pltpu.VMEM((GROUP, 2, HALF), F32),
            pltpu.VMEM((1, 2 * HALF), F32),
            pltpu.VMEM((1, 2 * HALF), F32),
            pltpu.VMEM((GROUP, 1, 2 * HALF), F32),
            pltpu.VMEM((HALF, 128), F32),
            pltpu.SMEM((R,), jnp.int32),
            pltpu.VMEM((HALF, E), BF16),
            pltpu.VMEM((HALF, E), BF16),
            pltpu.VMEM((HALF, E), BF16),
            pltpu.VMEM((HALF, E), BF16),
            pltpu.VMEM((2, 2, 2, RING, H, E), BF16),
            pltpu.VMEM((2, 2, 2, RING, H, E), BF16),
            dma((3,)),
            dma((2,)), dma((2, 2, 2, RING)),
            dma(()), dma(()),
            dma(()), dma(()),
            dma(()), dma(()),
            dma(()), dma(()),
            dma(()), dma(()),
            dma((2,)), dma((2, 2, 2, RING)),
        ],
        compiler_params=pltpu.CompilerParams(
            collective_id=0, has_side_effects=True, vmem_limit_bytes=40 * 1024 * 1024
        ),
        cost_estimate=pl.CostEstimate(flops=3221225472, bytes_accessed=262144, transcendentals=2097152),
        name="contrastive",
    )(image_emb, text_emb, labels, logit_scale.reshape(1))


def solution(mesh):
    in_specs = (P(("blk", "dp"), None), P(("blk", "dp"), None), P(("blk", "dp")), P())
    out_specs = (P(("blk", "dp"), None), P(("blk", "dp"), None))
    return jax.shard_map(
        per_device, mesh=mesh, in_specs=in_specs, out_specs=out_specs, check_vma=False
    )
```

time: 70.1 us -> 65.1 us (0.929)
  Pallas kernels: 64.6 us -> 59.3 us
    pallas_call x1, Pallas kernels: 64.6 us -> 59.3 us  [per_device(): pl.pallas_call(kernel, out_shape=(out, out), in_specs=[hbm, hbm, hbm, sme...]
where the time goes in v3:
time: 65.1 us; the launch traced here: 64.2 us
  Pallas kernels  59.3 us (91%)
  local copies, waits for them, and re-layouts  3.59 us (6%)
  between operations  1.3 us (2%)
    pallas_call x1, Pallas kernels, per_device(): pl.pallas_call(kernel, out_shape=(out, out), in_specs=[hbm, hbm, hbm, sme...  59.3 us
    unnamed x8, local copies, waits for them, and re-layouts  3.59 us

profile of v3, /device:TPU:1, one launch (start us, length us, event | category | flops | bytes accessed | tf_op | source)
XLA Modules:
  0.0 64.2 jit_solution(12135052763869590145)
XLA Ops:
  1.3 0.0 copy-start.2
  1.3 0.6 %copy-done.2 = s32[32]{0:T(128)S(1)} copy-done((s32[32]{0:T(128)S(1)}, s32[32]{0:T(128)}, u32[]{:S(2)}) %copy-start.2) | copy-done | bytes 152
  1.9 0.0 copy-start
  1.9 0.8 %copy-done = bf16[32,1024]{1,0:T(8,128)(2,1)S(1)} copy-done((bf16[32,1024]{1,0:T(8,128)(2,1)S(1)}, bf16[32,1024]{1,0:T(8,128)(2,1)}, u32[]{:S(2)}) %copy-start) | copy-done | bytes 65560
  2.8 0.0 copy-start.1
  2.8 0.8 %copy-done.1 = bf16[32,1024]{1,0:T(8,128)(2,1)S(1)} copy-done((bf16[32,1024]{1,0:T(8,128)(2,1)S(1)}, bf16[32,1024]{1,0:T(8,128)(2,1)}, u32[]{:S(2)}) %copy-start.1) | copy-done | bytes 65560
  3.6 59.3 %contrastive.1 = (bf16[32,1024]{1,0:T(8,128)(2,1)S(1)}, bf16[32,1024]{1,0:T(8,128)(2,1)S(1)}) custom-call(bf16[32,1024]{1,0:T(8,128)(2,1)S(1)} %copy-done, bf16[32,1024]{1,0:T(8,128)(2,1)S(1)} %copy-done.1, s32[32]{0:T(128)S(1)} %copy-done.2, f32[1]{0:T(128)} %bitcast.1.scale_ref), custom_call_target="tpu_custom_call" | custom-call | flops 3221225472 | bytes 262144 | tf_op jit(solution)/shard_map/contrastive/pallas_call | solution.py:323
  63.0 0.6 copy.9
  63.6 0.6 copy.10
Async XLA Ops:
  1.3 0.7 %copy-start.2 = (s32[32]{0:T(128)S(1)}, s32[32]{0:T(128)}, u32[]{:S(2)}) copy-start(s32[32]{0:T(128)} %label_ref.1) | copy-start | bytes 388
  1.9 0.8 %copy-start = (bf16[32,1024]{1,0:T(8,128)(2,1)S(1)}, bf16[32,1024]{1,0:T(8,128)(2,1)}, u32[]{:S(2)}) copy-start(bf16[32,1024]{1,0:T(8,128)(2,1)} %image_ref.1) | copy-start | bytes 196612
  2.8 0.8 %copy-start.1 = (bf16[32,1024]{1,0:T(8,128)(2,1)S(1)}, bf16[32,1024]{1,0:T(8,128)(2,1)}, u32[]{:S(2)}) copy-start(bf16[32,1024]{1,0:T(8,128)(2,1)} %text_ref.1) | copy-start | bytes 196612

commit v4 on v3

--- a/solution.py
+++ b/solution.py
@@ -181,9 +181,9 @@
         own_labels = jnp.where(at_label == r, labels[r], own_labels)
     row_ring[0, 1:2, :] = own_labels.astype(F32)
 
-    @pl.loop(0, 4)
+    @pl.loop(0, 2)
     def _(n):
-        @pl.when(n == 2)
+        @pl.when(n == 1)
         def _():
             arrived(col_sib, stat_send, stat_recv)
             from_sibling = col_sib[...]
@@ -192,11 +192,11 @@
             for k in range(1, GROUP):
                 send(col_ring.at[0], col_ring.at[k], scol_send, scol_recv, text_peers[k])
 
-        rows = pl.ds(pl.multiple_of(n * 128, 128), 128)
+        rows = pl.ds(pl.multiple_of(n * 256, 256), 256)
         tile = logits[rows, :]
         top = jnp.max(tile, axis=1, keepdims=True)
         total = jnp.sum(jnp.exp(tile - top), axis=1, keepdims=True)
-        row_stat[rows, :] = jnp.broadcast_to(top + jnp.log(total), (128, 128))
+        row_stat[rows, :] = jnp.broadcast_to(top + jnp.log(total), (256, 128))
 
     row_ring[0, 0:1, :] = jnp.transpose(row_stat[...])[0:1, :]
     for k in range(1, GROUP):
@@ -230,9 +230,9 @@
     left(col_ring.at[others], scol_send, scol_recv)
     left(row_ring.at[others], srow_send, srow_recv)
 
-    @pl.loop(0, 4)
+    @pl.loop(0, 2)
     def _(n):
-        rows = pl.ds(pl.multiple_of(n * 128, 128), 128)
+        rows = pl.ds(pl.multiple_of(n * 256, 256), 256)
         at_lane = lax.broadcasted_iota(jnp.int32, (1, 2 * HALF), 1)
         member = (at_lane >> 5) & 15
         its_y, parity = member >> 1, member & 1
@@ -248,14 +248,6 @@
         wts[rows, :] = weight.astype(BF16)
         wts_t[:, rows] = jnp.transpose(weight).astype(BF16)
 
-    @pl.loop(0, 4)
-    def _(n):
-        cols = pl.ds(pl.multiple_of(n * 256, 256), 256)
-        swap_out[:, cols] = jnp.dot(
-            wts_t[HALF:, :], images[:, cols], preferred_element_type=F32
-        ).astype(BF16)
-        send(swap_out.at[:, cols], swap_in.at[:, cols], swap_send, swap_recv, sibling)
-
     def summed(kind, piece):
         total = (grad_i if kind == 0 else grad_t)[piece_rows(kind, piece), :]
         for child in CHILDREN.get(piece, ()):
@@ -273,34 +265,47 @@
             out = (grad_i16 if kind == 0 else grad_t16).at[piece_rows(kind, piece)]
         send(out, landed.at[i], rs_send.at[kind], rs_recv.at[i], peer_of(kind, -parent(piece)[1]))
 
-    leaves = [piece for piece in BACKWARDS if piece not in CHILDREN]
-
-    @pl.loop(0, 4)
-    def _(n):
-        cols = pl.ds(pl.multiple_of(n * 256, 256), 256)
-        term = jnp.dot(wts[...], texts[:, cols], preferred_element_type=F32)
-        grad_i[:, cols] = term
-        grad_i16[:, cols] = term.astype(BF16)
-
-    for piece in leaves:
-        pass_on(0, piece)
-
-    @pl.loop(0, 4)
-    def _(n):
-        cols = pl.ds(pl.multiple_of(n * 256, 256), 256)
-        grad_t[:, cols] = jnp.dot(wts_t[:HALF, :], images[:, cols], preferred_element_type=F32)
-
-    arrived(swap_in, swap_send, swap_recv)
-
-    @pl.loop(0, 8)
-    def _(n):
-        rows = pl.ds(pl.multiple_of(n * 64, 64), 64)
-        term = grad_t[rows, :] + swap_in[rows, :].astype(F32)
-        grad_t[rows, :] = term
-        grad_t16[rows, :] = term.astype(BF16)
-
-    for piece in leaves:
-        pass_on(1, piece)
+    def band(kind, d, start=0):
+        return pl.ds(pl.multiple_of(along(place[kind], -d) * 2 * R + start, 2 * R), 2 * R)
+
+    def parts(term, bands):
+        return [(d, term[n * 2 * R : (n + 1) * 2 * R, :]) for n, d in enumerate(bands)]
+
+    def sibling_bands(bands):
+        left_side = jnp.concatenate([wts_t[band(1, d, HALF), :] for d in bands], axis=0)
+        term = jnp.dot(left_side, images[...], preferred_element_type=F32)
+        for d, part in parts(term, bands):
+            rows = band(1, d)
+            swap_out[rows, :] = part.astype(BF16)
+            theirs = swap_recv.at[(d if d == 4 else -d) + 3]
+            send(swap_out.at[rows], swap_in.at[rows], swap_send, theirs, sibling)
+
+    def image_bands(bands):
+        left_side = jnp.concatenate([wts[band(0, d), :] for d in bands], axis=0)
+        term = jnp.dot(left_side, texts[...], preferred_element_type=F32)
+        for d, part in parts(term, bands):
+            grad_i[band(0, d), :] = part
+            grad_i16[band(0, d), :] = part.astype(BF16)
+
+    def text_bands(bands):
+        left_side = jnp.concatenate([wts_t[band(1, d), :] for d in bands], axis=0)
+        term = jnp.dot(left_side, images[...], preferred_element_type=F32)
+        for d, part in parts(term, bands):
+            rows = band(1, d)
+            arrived(swap_in.at[rows], swap_send, swap_recv.at[d + 3])
+            total = part + swap_in[rows, :].astype(F32)
+            grad_t[rows, :] = total
+            grad_t16[rows, :] = total.astype(BF16)
+
+    for bands in ((4, 3, -3), (2, -2, 1, -1, 0)):
+        leaves = [piece for piece in BACKWARDS if piece not in CHILDREN and piece[2] in bands]
+        sibling_bands(bands)
+        image_bands(bands)
+        for piece in leaves:
+            pass_on(0, piece)
+        text_bands(bands)
+        for piece in leaves:
+            pass_on(1, piece)
     for piece in BACKWARDS:
         if piece in CHILDREN:
             for kind in range(2):
@@ -309,9 +314,9 @@
         for h in range(2):
             out_ref[pl.ds(h * H, H), :] = (scale * summed(kind, (0, h, 0))).astype(BF16)
 
-    left(swap_out, swap_send, swap_recv)
-    left(grad_i16.at[gathered], rs_send.at[0], swap_recv)
-    left(grad_t16.at[gathered], rs_send.at[1], swap_recv)
+    left(swap_out, swap_send, swap_recv.at[0])
+    left(grad_i16.at[gathered], rs_send.at[0], swap_recv.at[0])
+    left(grad_t16.at[gathered], rs_send.at[1], swap_recv.at[0])
 
 
 def per_device(image_emb, text_emb, labels, logit_scale):
@@ -353,7 +358,7 @@
             dma(()), dma(()),
             dma(()), dma(()),
             dma(()), dma(()),
-            dma(()), dma(()),
+            dma(()), dma((RING,)),
             dma((2,)), dma((2, 2, 2, RING)),
         ],
         compiler_params=pltpu.CompilerParams(

time: 65.1 us -> 64 us (0.983); the launches traced: 64.2 us -> 63.8 us
  no operation moved by 1% of the time
where the time goes in v4:
time: 64 us; the launch traced here: 63.8 us
  Pallas kernels  58.9 us (92%)
  local copies, waits for them, and re-layouts  3.59 us (6%)
  between operations  1.3 us (2%)
    pallas_call x1, Pallas kernels, per_device(): pl.pallas_call(kernel, out_shape=(out, out), in_specs=[hbm, hbm, hbm, sme...  58.9 us
    unnamed x8, local copies, waits for them, and re-layouts  3.59 us

profile of v4, /device:TPU:1, one launch (start us, length us, event | category | flops | bytes accessed | tf_op | source)
XLA Modules:
  0.0 63.8 jit_solution(2223580721834252027)
XLA Ops:
  1.3 0.0 copy-start.2
  1.3 0.6 %copy-done.2 = s32[32]{0:T(128)S(1)} copy-done((s32[32]{0:T(128)S(1)}, s32[32]{0:T(128)}, u32[]{:S(2)}) %copy-start.2) | copy-done | bytes 152
  1.9 0.0 copy-start
  1.9 0.8 %copy-done = bf16[32,1024]{1,0:T(8,128)(2,1)S(1)} copy-done((bf16[32,1024]{1,0:T(8,128)(2,1)S(1)}, bf16[32,1024]{1,0:T(8,128)(2,1)}, u32[]{:S(2)}) %copy-start) | copy-done | bytes 65560
  2.8 0.0 copy-start.1
  2.8 0.8 %copy-done.1 = bf16[32,1024]{1,0:T(8,128)(2,1)S(1)} copy-done((bf16[32,1024]{1,0:T(8,128)(2,1)S(1)}, bf16[32,1024]{1,0:T(8,128)(2,1)}, u32[]{:S(2)}) %copy-start.1) | copy-done | bytes 65560
  3.6 58.9 %contrastive.1 = (bf16[32,1024]{1,0:T(8,128)(2,1)S(1)}, bf16[32,1024]{1,0:T(8,128)(2,1)S(1)}) custom-call(bf16[32,1024]{1,0:T(8,128)(2,1)S(1)} %copy-done, bf16[32,1024]{1,0:T(8,128)(2,1)S(1)} %copy-done.1, s32[32]{0:T(128)S(1)} %copy-done.2, f32[1]{0:T(128)} %bitcast.1.scale_ref), custom_call_target="tpu_custom_call" | custom-call | flops 3221225472 | bytes 262144 | tf_op jit(solution)/shard_map/contrastive/pallas_call | solution.py:328
  62.5 0.6 copy.9
  63.2 0.6 copy.10
Async XLA Ops:
  1.3 0.7 %copy-start.2 = (s32[32]{0:T(128)S(1)}, s32[32]{0:T(128)}, u32[]{:S(2)}) copy-start(s32[32]{0:T(128)} %label_ref.1) | copy-start | bytes 388
  1.9 0.8 %copy-start = (bf16[32,1024]{1,0:T(8,128)(2,1)S(1)}, bf16[32,1024]{1,0:T(8,128)(2,1)}, u32[]{:S(2)}) copy-start(bf16[32,1024]{1,0:T(8,128)(2,1)} %image_ref.1) | copy-start | bytes 196612
  2.8 0.8 %copy-start.1 = (bf16[32,1024]{1,0:T(8,128)(2,1)S(1)}, bf16[32,1024]{1,0:T(8,128)(2,1)}, u32[]{:S(2)}) copy-start(bf16[32,1024]{1,0:T(8,128)(2,1)} %text_ref.1) | copy-start | bytes 196612

commit v5 on v4

--- a/solution.py
+++ b/solution.py
@@ -143,6 +143,12 @@
     for piece in STAGES[0]:
         for kind in range(2):
             gather_send(kind, piece)
+    at_label = lax.broadcasted_iota(jnp.int32, (1, HALF), 1) - (z * 2 + p) * R
+    own_labels = jnp.zeros((1, HALF), jnp.int32)
+    for r in range(R):
+        own_labels = jnp.where(at_label == r, labels[r], own_labels)
+    row_ring[0, 1:2, :] = own_labels.astype(F32)
+
     got = {(0, 0, 0), (0, 1, 0)}
     for pieces in STAGES:
         for piece in pieces:
@@ -175,12 +181,6 @@
 
     send(col_vec, col_sib, stat_send, stat_recv, sibling)
 
-    at_label = lax.broadcasted_iota(jnp.int32, (1, HALF), 1) - (z * 2 + p) * R
-    own_labels = jnp.zeros((1, HALF), jnp.int32)
-    for r in range(R):
-        own_labels = jnp.where(at_label == r, labels[r], own_labels)
-    row_ring[0, 1:2, :] = own_labels.astype(F32)
-
     @pl.loop(0, 2)
     def _(n):
         @pl.when(n == 1)
@@ -230,9 +230,9 @@
     left(col_ring.at[others], scol_send, scol_recv)
     left(row_ring.at[others], srow_send, srow_recv)
 
-    @pl.loop(0, 2)
+    @pl.loop(0, 1)
     def _(n):
-        rows = pl.ds(pl.multiple_of(n * 256, 256), 256)
+        rows = pl.ds(pl.multiple_of(n * 512, 512), 512)
         at_lane = lax.broadcasted_iota(jnp.int32, (1, 2 * HALF), 1)
         member = (at_lane >> 5) & 15
         its_y, parity = member >> 1, member & 1
@@ -312,7 +312,7 @@
                 pass_on(kind, piece)
     for kind, out_ref in ((0, out_image_ref), (1, out_text_ref)):
         for h in range(2):
-            out_ref[pl.ds(h * H, H), :] = (scale * summed(kind, (0, h, 0))).astype(BF16)
+            out_ref[pl.ds(h * H, H), :] = scale * summed(kind, (0, h, 0))
 
     left(swap_out, swap_send, swap_recv.at[0])
     left(grad_i16.at[gathered], rs_send.at[0], swap_recv.at[0])
@@ -324,8 +324,8 @@
     smem = pl.BlockSpec(memory_space=pltpu.SMEM)
     hbm = pl.BlockSpec(memory_space=pltpu.HBM)
     dma = pltpu.SemaphoreType.DMA
-    out = jax.ShapeDtypeStruct((R, E), BF16)
-    return pl.pallas_call(
+    out = jax.ShapeDtypeStruct((R, E), F32)
+    grads = pl.pallas_call(
         kernel,
         out_shape=(out, out),
         in_specs=[hbm, hbm, hbm, smem],
@@ -362,11 +362,12 @@
             dma((2,)), dma((2, 2, 2, RING)),
         ],
         compiler_params=pltpu.CompilerParams(
-            collective_id=0, has_side_effects=True, vmem_limit_bytes=40 * 1024 * 1024
+            collective_id=0, has_side_effects=True, vmem_limit_bytes=56 * 1024 * 1024
         ),
         cost_estimate=pl.CostEstimate(flops=3221225472, bytes_accessed=262144, transcendentals=2097152),
         name="contrastive",
     )(image_emb, text_emb, labels, logit_scale.reshape(1))
+    return tuple(grad.astype(BF16) for grad in grads)
 
 
 def solution(mesh):

time: 64 us -> 63.1 us (0.986)
  local copies, waits for them, and re-layouts: 3.59 us -> 0.01 us
  other arithmetic: 0 us -> 2.21 us
    unnamed x8 -> x2, local copies, waits for them, and re-layouts: 3.59 us -> 0.01 us
    convert_element_type x0 -> x2, other arithmetic: none -> 2.21 us  [per_device(): return tuple((grad.astype(BF16) for grad in grads))]
where the time goes in v5:
time: 63.1 us; the launch traced here: 62.9 us
  Pallas kernels  59.4 us (94%)
  other arithmetic  2.21 us (4%)
  between operations  1.29 us (2%)
    pallas_call x1, Pallas kernels, per_device(): pl.pallas_call(kernel, out_shape=(out, out), in_specs=[hbm, hbm, hbm, sme...  59.4 us
    convert_element_type x2, other arithmetic, per_device(): return tuple((grad.astype(BF16) for grad in grads))  2.21 us

profile of v5, /device:TPU:1, one launch (start us, length us, event | category | flops | bytes accessed | tf_op | source)
XLA Modules:
  0.0 62.9 jit_solution(12735581296651645387)
XLA Ops:
  1.3 59.4 %contrastive.1 = (f32[32,1024]{1,0:T(8,128)}, f32[32,1024]{1,0:T(8,128)}) custom-call(bf16[32,1024]{1,0:T(8,128)(2,1)} %image_ref.1, bf16[32,1024]{1,0:T(8,128)(2,1)} %text_ref.1, s32[32]{0:T(128)} %label_ref.1, f32[1]{0:T(128)} %bitcast.1.scale_ref), custom_call_target="tpu_custom_call" | custom-call | flops 3221225472 | bytes 262144 | tf_op jit(solution)/shard_map/contrastive/pallas_call | solution.py:328
  60.6 0.0 copy-start
  60.7 1.6 %convert_element_type.6 = bf16[32,1024]{1,0:T(8,128)(2,1)} convert(f32[32,1024]{1,0:T(8,128)} %get-tuple-element.4) | non-fusion elementwise | flops 32768 | bytes 196608 | tf_op jit(solution)/shard_map/convert_element_type | solution.py:370
  62.2 0.0 copy-done
  62.2 0.6 %convert_element_type.7 = bf16[32,1024]{1,0:T(8,128)(2,1)} convert(f32[32,1024]{1,0:T(8,128)S(1)} %copy-done) | non-fusion elementwise | flops 32768 | bytes 196608 | tf_op jit(solution)/shard_map/convert_element_type | solution.py:370
Async XLA Ops:
  60.6 1.6 %copy-start = (f32[32,1024]{1,0:T(8,128)S(1)}, f32[32,1024]{1,0:T(8,128)}, u32[]{:S(2)}) copy-start(f32[32,1024]{1,0:T(8,128)} %get-tuple-element.5) | copy-start | bytes 393220

commit v6 on v5

--- a/solution.py
+++ b/solution.py
@@ -30,7 +30,7 @@
 
 def parent(piece):
     q, h, d = piece
-    if q == 1 and (h == 1 or d == 0):
+    if q == 1 and (h == 1 or abs(d) < 2):
         return (0, h, d), 0
     if d == 4:
         step = -2 if (q, h) == (0, 1) else 2

time: 63.1 us -> 62.8 us (level)
  no operation moved by 1% of the time
where the time goes in v6:
time: 62.8 us; the launch traced here: 62.7 us
  Pallas kernels  59.1 us (94%)
  other arithmetic  2.21 us (4%)
  between operations  1.29 us (2%)
    pallas_call x1, Pallas kernels, per_device(): pl.pallas_call(kernel, out_shape=(out, out), in_specs=[hbm, hbm, hbm, sme...  59.1 us
    convert_element_type x2, other arithmetic, per_device(): return tuple((grad.astype(BF16) for grad in grads))  2.21 us

profile of v6, /device:TPU:1, one launch (start us, length us, event | category | flops | bytes accessed | tf_op | source)
XLA Modules:
  0.0 62.7 jit_solution(14065827710651854497)
XLA Ops:
  1.3 59.1 %contrastive.1 = (f32[32,1024]{1,0:T(8,128)}, f32[32,1024]{1,0:T(8,128)}) custom-call(bf16[32,1024]{1,0:T(8,128)(2,1)} %image_ref.1, bf16[32,1024]{1,0:T(8,128)(2,1)} %text_ref.1, s32[32]{0:T(128)} %label_ref.1, f32[1]{0:T(128)} %bitcast.1.scale_ref), custom_call_target="tpu_custom_call" | custom-call | flops 3221225472 | bytes 262144 | tf_op jit(solution)/shard_map/contrastive/pallas_call | solution.py:328
  60.4 0.0 copy-start
  60.4 1.6 %convert_element_type.6 = bf16[32,1024]{1,0:T(8,128)(2,1)} convert(f32[32,1024]{1,0:T(8,128)} %get-tuple-element.4) | non-fusion elementwise | flops 32768 | bytes 196608 | tf_op jit(solution)/shard_map/convert_element_type | solution.py:370
  62.0 0.0 copy-done
  62.0 0.6 %convert_element_type.7 = bf16[32,1024]{1,0:T(8,128)(2,1)} convert(f32[32,1024]{1,0:T(8,128)S(1)} %copy-done) | non-fusion elementwise | flops 32768 | bytes 196608 | tf_op jit(solution)/shard_map/convert_element_type | solution.py:370
Async XLA Ops:
  60.4 1.6 %copy-start = (f32[32,1024]{1,0:T(8,128)S(1)}, f32[32,1024]{1,0:T(8,128)}, u32[]{:S(2)}) copy-start(f32[32,1024]{1,0:T(8,128)} %get-tuple-element.5) | copy-start | bytes 393220
